TPU v7x, 32 devices: a whole 2x2x4 slice. The times are simulated.
32 devices in a mesh: shard: 4 (over z), rep: 8 (over y, x, core).
Axes of the slice: x: 2, y: 2, z: 4, core: 2. Of those that a mesh axis runs over, the one named last changes fastest.
Arguments:
- latents_in: bfloat16 [65536, 384], P(('shard', 'rep')), may hold values from -6 to 6
- conditioning: bfloat16 [256, 384], P(('shard', 'rep')), may hold values from -6 to 6
- ada_weight: bfloat16 [384, 2304], P('shard'), may hold values from -0.3125 to 0.3125
- ada_bias: bfloat16 [2304], P('shard'), may hold values from -1.796875 to 1.796875
- qkv_weight: bfloat16 [384, 1152], P('shard'), may hold values from -0.3125 to 0.3125
- qv_bias: bfloat16 [768], P('shard'), may hold values from -1.796875 to 1.796875
- proj_weight: bfloat16 [384, 384], P('shard'), may hold values from -1.25 to 1.25
- proj_bias: bfloat16 [384], P('shard'), may hold values from -1.796875 to 1.796875
- fc1_weight: bfloat16 [384, 1536], P('shard'), may hold values from -0.3125 to 0.3125
- fc1_bias: bfloat16 [1536], P('shard'), may hold values from -1.796875 to 1.796875
- fc2_weight: bfloat16 [1536, 384], P('shard'), may hold values from -0.15625 to 0.15625
- fc2_bias: bfloat16 [384], P('shard'), may hold values from -1.796875 to 1.796875
- cotangent: bfloat16 [65536, 384], P(('shard', 'rep')), may hold values from -6 to 6
Outputs:
- layer_out: bfloat16 [65536, 384], P(('shard', 'rep'))
- grad_latents: float32 [65536, 384], P(('shard', 'rep'))
- grad_conditioning: float32 [256, 384], P(('shard', 'rep'))
- grad_ada_weight: float32 [384, 2304], P('shard')
- grad_ada_bias: float32 [2304], P('shard')
- grad_qkv_weight: float32 [384, 1152], P('shard')
- grad_qv_bias: float32 [768], P('shard')
- grad_proj_weight: float32 [384, 384], P('shard')
- grad_proj_bias: float32 [384], P('shard')
- grad_fc1_weight: float32 [384, 1536], P('shard')
- grad_fc1_bias: float32 [1536], P('shard')
- grad_fc2_weight: float32 [1536, 384], P('shard')
- grad_fc2_bias: float32 [384], P('shard')
All inputs are finite; a program needn't handle non-finite values.
Results may differ from a plain program's by a relative error of at most 0.01.
The roundings to bfloat16 on the way count: a program that leaves them out, or rounds other values in their place, can miss the bound.
Values may be sent and summed in bfloat16 or wider, within the bound.
A program may use at most 128 MiB of HBM per device.

v0:
```python
import jax
import jax.numpy as jnp
from jax import lax
from jax.sharding import PartitionSpec as P

HEAD_DIM = 64


EPSILON = 1e-06


def layer_norm(values):
    center = values - jnp.mean(values, axis=-1, keepdims=True)
    spread = jnp.mean(center * center, axis=-1, keepdims=True)
    return center * lax.rsqrt(spread + EPSILON)


def modulate(values, shift_rows, scale_rows):
    return layer_norm(values) * (1.0 + scale_rows[:, None, :]) + shift_rows[:, None, :]


def gelu_tanh(values):
    return jax.nn.gelu(values, approximate=True)


def project(inputs, weight):
    return jnp.einsum("lsd,de->lse", inputs, weight, preferred_element_type=jnp.float32)


def project_back(gradient, weight):
    return jnp.einsum("lse,de->lsd", gradient, weight, preferred_element_type=jnp.float32)


def weight_grad(inputs, gradient):
    return jnp.einsum("lsd,lse->de", inputs, gradient, preferred_element_type=jnp.float32)


def column_sums(gradient):
    return jnp.sum(gradient, axis=(0, 1), dtype=jnp.float32)


def shards(
    latents_in,
    conditioning,
    ada_weight,
    ada_bias,
    qkv_weight,
    qv_bias,
    proj_weight,
    proj_bias,
    fc1_weight,
    fc1_bias,
    fc2_weight,
    fc2_bias,
    cotangent,
):
    latent_count = conditioning.shape[0]
    model_width = conditioning.shape[1]
    seq_length = latents_in.shape[0] // latent_count
    head_count = model_width // HEAD_DIM
    softmax_scale = HEAD_DIM ** (-0.5)
    (
        mod_weight,
        mod_bias,
        qkv_matrix,
        qv_offsets,
        proj_matrix,
        proj_offsets,
        up_matrix,
        up_offsets,
        down_matrix,
        down_offsets,
    ) = (
        lax.all_gather(ada_weight, "shard", axis=0, tiled=True),
        lax.all_gather(ada_bias, "shard", axis=0, tiled=True),
        lax.all_gather(qkv_weight, "shard", axis=0, tiled=True),
        lax.all_gather(qv_bias, "shard", axis=0, tiled=True),
        lax.all_gather(proj_weight, "shard", axis=0, tiled=True),
        lax.all_gather(proj_bias, "shard", axis=0, tiled=True),
        lax.all_gather(fc1_weight, "shard", axis=0, tiled=True),
        lax.all_gather(fc1_bias, "shard", axis=0, tiled=True),
        lax.all_gather(fc2_weight, "shard", axis=0, tiled=True),
        lax.all_gather(fc2_bias, "shard", axis=0, tiled=True),
    )
    inputs = latents_in.astype(jnp.float32).reshape(latent_count, seq_length, model_width)
    cond_silu, silu_pull = jax.vjp(jax.nn.silu, conditioning.astype(jnp.float32))
    silu_low = cond_silu.astype(jnp.bfloat16)
    modulation = jnp.dot(
        silu_low, mod_weight, preferred_element_type=jnp.float32
    ) + mod_bias.astype(jnp.float32)
    shift_one, scale_one, gate_one, shift_two, scale_two, gate_two = jnp.split(
        modulation, 6, axis=1
    )
    first_in, first_pull = jax.vjp(modulate, inputs, shift_one, scale_one)
    first_low = first_in.astype(jnp.bfloat16)
    zero_bias = jnp.zeros((model_width,), jnp.bfloat16)
    full_bias = jnp.concatenate(
        [qv_offsets[:model_width], zero_bias, qv_offsets[model_width:]]
    ).astype(jnp.float32)
    qkv_low = (project(first_low, qkv_matrix) + full_bias).astype(jnp.bfloat16)
    qkv_low = qkv_low.reshape(latent_count, seq_length, 3, head_count, HEAD_DIM)
    queries = qkv_low[:, :, 0]
    key_rows = qkv_low[:, :, 1]
    value_rows = qkv_low[:, :, 2]
    scores = (
        jnp.einsum("lqhd,lkhd->lhqk", queries, key_rows, preferred_element_type=jnp.float32)
        * softmax_scale
    )
    row_max = jnp.max(scores, axis=-1, keepdims=True)
    log_total = row_max + jnp.log(jnp.sum(jnp.exp(scores - row_max), axis=-1, keepdims=True))
    probs_fwd = jnp.exp(scores - log_total).astype(jnp.bfloat16)
    attended = jnp.einsum(
        "lhqk,lkhd->lqhd", probs_fwd, value_rows, preferred_element_type=jnp.float32
    )
    attended_low = attended.reshape(latent_count, seq_length, model_width).astype(jnp.bfloat16)
    attn_out = project(attended_low, proj_matrix) + proj_offsets.astype(jnp.float32)
    middle = inputs + gate_one[:, None, :] * attn_out
    second_in, second_pull = jax.vjp(modulate, middle, shift_two, scale_two)
    second_low = second_in.astype(jnp.bfloat16)
    hidden_pre = project(second_low, up_matrix) + up_offsets.astype(jnp.float32)
    hidden_act, gelu_pull = jax.vjp(gelu_tanh, hidden_pre)
    hidden_low = hidden_act.astype(jnp.bfloat16)
    branch_out = project(hidden_low, down_matrix) + down_offsets.astype(jnp.float32)
    result = middle + gate_two[:, None, :] * branch_out
    (
        mod_weight,
        mod_bias,
        qkv_matrix,
        qv_offsets,
        proj_matrix,
        proj_offsets,
        up_matrix,
        up_offsets,
        down_matrix,
        down_offsets,
    ) = (
        lax.all_gather(ada_weight, "shard", axis=0, tiled=True),
        lax.all_gather(ada_bias, "shard", axis=0, tiled=True),
        lax.all_gather(qkv_weight, "shard", axis=0, tiled=True),
        lax.all_gather(qv_bias, "shard", axis=0, tiled=True),
        lax.all_gather(proj_weight, "shard", axis=0, tiled=True),
        lax.all_gather(proj_bias, "shard", axis=0, tiled=True),
        lax.all_gather(fc1_weight, "shard", axis=0, tiled=True),
        lax.all_gather(fc1_bias, "shard", axis=0, tiled=True),
        lax.all_gather(fc2_weight, "shard", axis=0, tiled=True),
        lax.all_gather(fc2_bias, "shard", axis=0, tiled=True),
    )
    upstream = cotangent.astype(jnp.float32).reshape(latent_count, seq_length, model_width)
    down_grad = (gate_two[:, None, :] * upstream).astype(jnp.bfloat16)
    gate_two_grad = jnp.sum(upstream * branch_out, axis=1)
    down_w_grad = weight_grad(hidden_low, down_grad)
    down_b_grad = column_sums(down_grad)
    hidden_grad = gelu_pull(project_back(down_grad, down_matrix))[0].astype(jnp.bfloat16)
    up_w_grad = weight_grad(second_low, hidden_grad)
    up_b_grad = column_sums(hidden_grad)
    middle_part, shift_two_grad, scale_two_grad = second_pull(project_back(hidden_grad, up_matrix))
    middle_grad = upstream + middle_part
    attn_grad = (gate_one[:, None, :] * middle_grad).astype(jnp.bfloat16)
    gate_one_grad = jnp.sum(middle_grad * attn_out, axis=1)
    proj_w_grad = weight_grad(attended_low, attn_grad)
    proj_b_grad = column_sums(attn_grad)
    attended_grad = project_back(attn_grad, proj_matrix).astype(jnp.bfloat16)
    attended_grad = attended_grad.reshape(latent_count, seq_length, head_count, HEAD_DIM)
    scores_again = (
        jnp.einsum("lqhd,lkhd->lhqk", queries, key_rows, preferred_element_type=jnp.float32)
        * softmax_scale
    )
    probs_again = jnp.exp(scores_again - log_total)
    value_grad = jnp.einsum(
        "lhqk,lqhd->lkhd",
        probs_again.astype(jnp.bfloat16),
        attended_grad,
        preferred_element_type=jnp.float32,
    )
    probs_grad = jnp.einsum(
        "lqhd,lkhd->lhqk", attended_grad, value_rows, preferred_element_type=jnp.float32
    )
    score_grad = probs_again * (
        probs_grad - jnp.sum(probs_again * probs_grad, axis=-1, keepdims=True)
    )
    score_low = score_grad.astype(jnp.bfloat16)
    query_grad = (
        jnp.einsum("lhqk,lkhd->lqhd", score_low, key_rows, preferred_element_type=jnp.float32)
        * softmax_scale
    )
    key_grad = (
        jnp.einsum("lhqk,lqhd->lkhd", score_low, queries, preferred_element_type=jnp.float32)
        * softmax_scale
    )
    qkv_grad = jnp.stack([query_grad, key_grad, value_grad], axis=2)
    qkv_grad = qkv_grad.reshape(latent_count, seq_length, 3 * model_width).astype(jnp.bfloat16)
    qkv_w_grad = weight_grad(first_low, qkv_grad)
    qkv_sums = column_sums(qkv_grad)
    qv_b_grad = jnp.concatenate([qkv_sums[:model_width], qkv_sums[2 * model_width :]])
    input_part, shift_one_grad, scale_one_grad = first_pull(project_back(qkv_grad, qkv_matrix))
    input_grad = middle_grad + input_part
    mod_grad = jnp.concatenate(
        [
            shift_one_grad,
            scale_one_grad,
            gate_one_grad,
            shift_two_grad,
            scale_two_grad,
            gate_two_grad,
        ],
        axis=1,
    ).astype(jnp.bfloat16)
    ada_w_grad = jnp.einsum("ld,le->de", silu_low, mod_grad, preferred_element_type=jnp.float32)
    ada_b_grad = jnp.sum(mod_grad, axis=0, dtype=jnp.float32)
    cond_grad = silu_pull(
        jnp.einsum("le,de->ld", mod_grad, mod_weight, preferred_element_type=jnp.float32)
    )[0]
    partials = (
        ada_w_grad,
        ada_b_grad,
        qkv_w_grad,
        qv_b_grad,
        proj_w_grad,
        proj_b_grad,
        up_w_grad,
        up_b_grad,
        down_w_grad,
        down_b_grad,
    )
    owned = (
        lax.psum_scatter(partials[0], "shard", scatter_dimension=0, tiled=True),
        lax.psum_scatter(partials[1], "shard", scatter_dimension=0, tiled=True),
        lax.psum_scatter(partials[2], "shard", scatter_dimension=0, tiled=True),
        lax.psum_scatter(partials[3], "shard", scatter_dimension=0, tiled=True),
        lax.psum_scatter(partials[4], "shard", scatter_dimension=0, tiled=True),
        lax.psum_scatter(partials[5], "shard", scatter_dimension=0, tiled=True),
        lax.psum_scatter(partials[6], "shard", scatter_dimension=0, tiled=True),
        lax.psum_scatter(partials[7], "shard", scatter_dimension=0, tiled=True),
        lax.psum_scatter(partials[8], "shard", scatter_dimension=0, tiled=True),
        lax.psum_scatter(partials[9], "shard", scatter_dimension=0, tiled=True),
    )
    finals = lax.psum(
        (
            owned[0],
            owned[1],
            owned[2],
            owned[3],
            owned[4],
            owned[5],
            owned[6],
            owned[7],
            owned[8],
            owned[9],
        ),
        "rep",
    )
    (
        final_ada_w,
        final_ada_b,
        final_qkv_w,
        final_qv_b,
        final_proj_w,
        final_proj_b,
        final_up_w,
        final_up_b,
        final_down_w,
        final_down_b,
    ) = finals
    return (
        result.reshape(latent_count * seq_length, model_width).astype(jnp.bfloat16),
        input_grad.reshape(latent_count * seq_length, model_width),
        cond_grad,
        final_ada_w,
        final_ada_b,
        final_qkv_w,
        final_qv_b,
        final_proj_w,
        final_proj_b,
        final_up_w,
        final_up_b,
        final_down_w,
        final_down_b,
    )


def solution(mesh):
    return jax.shard_map(
        shards,
        mesh=mesh,
        in_specs=(
            P(("shard", "rep"), None),
            P(("shard", "rep"), None),
            P("shard", None),
            P("shard"),
            P("shard", None),
            P("shard"),
            P("shard", None),
            P("shard"),
            P("shard", None),
            P("shard"),
            P("shard", None),
            P("shard"),
            P(("shard", "rep"), None),
        ),
        out_specs=(
            P(("shard", "rep"), None),
            P(("shard", "rep"), None),
            P(("shard", "rep"), None),
            P("shard", None),
            P("shard"),
            P("shard", None),
            P("shard"),
            P("shard", None),
            P("shard"),
            P("shard", None),
            P("shard"),
            P("shard", None),
            P("shard"),
        ),
        check_vma=False,
    )
```

profile of v0, /device:TPU:0, one launch (start us, length us, event | category | flops | bytes accessed | tf_op | source)
XLA Modules:
  0.0 512.3 jit_solution(9304998192891519238)
XLA Ops:
  9.6 1.8 convert_reduce_fusion.4
  14.8 13.7 %all-gather = bf16[4,1,384]{2,1,0:T(2,128)(2,1)S(1)} all-gather(bf16[1,1,384]{2,1,0:T(2,128)(2,1)S(1)} %reshape.199), channel_id=1, replica_groups=mesh['shard'=4,'rep'=8] {'shard'}, dimensions={0}, use_global_device_ids=true | all-gather | bytes 3840 | tf_op jit(solution)/shard_map/all_gather | solution.py:81
  30.1 18.3 %all-reduce.12 = (bf16[768]{0:T(1024)(128)(2,1)S(1)}, bf16[2304]{0:T(1024)(128)(2,1)S(1)}, bf16[384]{0:T(512)(128)(2,1)S(1)}, bf16[384]{0:T(512)(128)(2,1)S(1)}) all-reduce(bf16[768]{0:T(1024)(128)(2,1)S(1)} %dynamic-update-slice.1, bf16[2304]{0:T(1024)(128)(2,1)S(1)} %dynamic-update-slice, ...), channel_id=1, replica_groups=mesh['shard'=4,'rep'=8] {'shard'}, use_global_device_ids=true, to_apply=%add.1 | all-reduce | flops 3840 | bytes 15360
  50.2 14.9 %all_gather.39 = bf16[384,384]{1,0:T(8,128)(2,1)S(1)} all-gather(bf16[96,384]{1,0:T(8,128)(2,1)S(1)} %copy-done.33), channel_id=1, replica_groups=mesh['shard'=4,'rep'=8] {'shard'}, dimensions={0}, use_global_device_ids=true | all-gather | bytes 368640 | tf_op jit(solution)/shard_map/all_gather | solution.py:78
  65.1 28.1 %all_gather.37 = bf16[384,1152]{1,0:T(8,128)(2,1)S(1)} all-gather(bf16[96,1152]{1,0:T(8,128)(2,1)S(1)} %copy-done.20), channel_id=1, replica_groups=mesh['shard'=4,'rep'=8] {'shard'}, dimensions={0}, use_global_device_ids=true | all-gather | bytes 1105920 | tf_op jit(solution)/shard_map/all_gather | solution.py:76
  93.2 2.1 convolution_add_fusion
  96.0 4.8 add_convert_fusion
  100.8 6.7 %copy.71 = bf16[8,256,1152]{1,2,0:T(8,128)(2,1)} copy(bf16[8,256,1152]{2,1,0:T(8,128)(2,1)} %add_convert_fusion) | data formatting | bytes 9437184 | tf_op jit(solution)/shard_map/convert_element_type | solution.py:100
  107.5 3.7 multiply_reduce_fusion.1
  111.2 2.6 exponential_reduce_fusion
  113.8 1.9 copy-done
  115.7 3.9 convolution_convert_fusion.1
  119.6 2.9 multiply_add_fusion
  124.2 10.7 %multiply_convert_fusion.1 = (bf16[8,256,1536]{2,1,0:T(8,128)(2,1)}, f32[8,256,1536]{2,1,0:T(8,128)}) fusion(f32[1536]{0:T(1024)} %reshape.201, bf16[384,1536]{1,0:T(8,128)(2,1)} %all-gather.7.cloned.1.call-done, f32[8,256,384]{2,1,0:T(8,128)S(1)} %get-tuple-element.64, f32[8,384]{1,0:T(8,128)S(1)} %get-tuple-element.49, ...), kind=kOutput, calls=%fused_computation.12 | convolution fusion | flops 2451308544 | bytes 23246848 | tf_op jit(solution)/shard_map/lsd,de->lse/dot_general | solution.py:27
  134.9 9.3 %multiply_reduce_fusion.2 = (bf16[8,384]{1,0:T(8,128)(2,1)}, f32[2048,384]{1,0:T(8,128)S(1)}, bf16[8,256,384]{2,1,0:T(8,128)(2,1)}) fusion(f32[384]{0:T(512)} %convert_element_type.132, bf16[2048,384]{1,0:T(8,128)(2,1)} %param.25, f32[8,256,384]{2,1,0:T(8,128)S(1)} %get-tuple-element.64, f32[8,384]{1,0:T(8,128)} %get-tuple-element.48, ...), kind=kOutput, calls=%fused_computation.30 | convolution fusion | flops 2421421056 | bytes 16928256 | tf_op jit(solution)/shard_map/lsd,de->lse/dot_general | solution.py:27
  144.3 14.6 %convert_reduce_fusion = (f32[1536]{0:T(1024)}, bf16[8,256,1536]{2,1,0:T(8,128)(2,1)S(1)}) fusion(f32[8,256,1536]{2,1,0:T(8,128)} %get-tuple-element.67, f32[1536]{0:T(1024)S(1)} %copy-done.47, bf16[1536,384]{1,0:T(8,128)(2,1)S(1)} %copy-done.53, f32[8,256,384]{2,1,0:T(8,128)S(1)} %bitcast.145, f32[8,384]{1,0:T(8,128)S(1)} %copy-done.36), kind=kOutput, calls=%fused_computation.9 | convolution fusion | flops 2489842176 | bytes 23224320 | tf_op jit(solution)/shard_map/lse,de->lsd/dot_general | solution.py:31
  158.9 3.7 multiply_reduce_fusion.7
  162.7 2.4 multiply_reduce_fusion.3
  165.1 3.6 convert_reduce_fusion.3
  168.6 1.2 copy-done.10
  169.8 1.8 convolution_bitcast_fusion.4
  171.6 3.7 convolution_convert_fusion
  175.2 2.6 copy.77
  177.8 8.6 %convolution_bitcast_fusion.3 = bf16[8,256,1,6,64]{1,4,3,0,2:T(8,128)(2,1)} fusion(bf16[8,256,6,64]{1,3,2,0:T(8,128)(2,1)} %bitcast.138, f32[8,6,256,256]{2,3,1,0:T(8,128)} %copy-done, f32[8,6,256]{2,1,0:T(8,128)S(1)} %log_add_fusion), kind=kOutput, calls=%fused_computation.52 | convolution fusion | flops 412090368 | bytes 15777792 | tf_op jit(solution)/shard_map/lhqk,lqhd->lkhd/dot_general | solution.py:169
  186.4 9.5 %multiply_reduce_fusion = (f32[8,6,256]{2,1,0:T(8,128)S(1)}, f32[8,6,256,256]{2,3,1,0:T(8,128)}) fusion(f32[8,6,256,256]{2,3,1,0:T(8,128)} %copy-done, f32[8,6,256]{2,1,0:T(8,128)S(1)} %log_add_fusion, bf16[8,256,6,64]{1,3,2,0:T(8,128)(2,1)S(1)} %bitcast.139, bf16[8,256,3,6,64]{1,4,3,2,0:T(8,128)(2,1)} %bitcast.135), kind=kOutput, calls=%fused_computation.11 | convolution fusion | flops 415223808 | bytes 28409856 | tf_op jit(solution)/shard_map/lqhd,lkhd->lhqk/dot_general | solution.py:175
  196.0 9.8 %multiply_convert_fusion = bf16[8,6,256,256]{2,3,1,0:T(8,128)(2,1)S(1)} fusion(f32[8,6,256,256]{2,3,1,0:T(8,128)} %get-tuple-element.71, f32[8,6,256,256]{2,3,1,0:T(8,128)} %copy-done, f32[8,6,256]{2,1,0:T(8,128)S(1)} %get-tuple-element.70, f32[8,6,256]{2,1,0:T(8,128)S(1)} %log_add_fusion), kind=kLoop, calls=%fused_computation.10 | loop fusion | flops 15728640 | bytes 31555584 | tf_op jit(solution)/shard_map/convert_element_type | solution.py:181
  205.8 3.4 multiply_bitcast_fusion
  209.3 2.7 multiply_bitcast_fusion.1
  213.5 1.0 convert_reduce_fusion.1
  215.2 2.1 copy-done.14
  217.3 3.5 convolution_bitcast_fusion.2
  220.9 8.6 %convolution_bitcast_fusion = f32[1536,384]{1,0:T(8,128)} fusion(bf16[8,256,1536]{2,1,0:T(8,128)(2,1)} %get-tuple-element.66, f32[8,256,384]{2,1,0:T(8,128)} %bitcast.146, f32[8,384]{1,0:T(8,128)S(1)} %copy-done.37), kind=kOutput, calls=%fused_computation.48 | convolution fusion | flops 2417491968 | bytes 11808768 | tf_op jit(solution)/shard_map/lsd,lse->de/dot_general | solution.py:35
  229.5 7.0 %convolution_bitcast_fusion.1 = f32[384,1536]{1,0:T(8,128)} fusion(bf16[8,256,1536]{2,1,0:T(8,128)(2,1)} %copy-done.5, f32[8,256,384]{2,1,0:T(8,128)S(1)} %get-tuple-element.64, f32[8,384]{1,0:T(8,128)S(1)} %get-tuple-element.49, f32[8,384]{1,0:T(8,128)S(1)} %get-tuple-element.50, f32[8,256]{1,0:T(8,128)S(1)} %fusion.39, ...), kind=kOutput, calls=%fused_computation.49 | convolution fusion | flops 2419851264 | bytes 11837440 | tf_op jit(solution)/shard_map/lsd,lse->de/dot_general | solution.py:35
  236.9 6.8 %multiply_reduce_fusion.6 = (f32[8,256]{1,0:T(8,128)S(1)}, f32[8,256,384]{2,1,0:T(8,128)S(1)}) fusion(f32[8,384]{1,0:T(8,128)S(1)} %copy-done.22, f32[8,256]{1,0:T(8,128)S(1)} %copy-done.26, bf16[8,256,1152]{1,2,0:T(8,128)(2,1)} %bitcast.143, bf16[384,1152]{1,0:T(8,128)(2,1)} %copy-done.17, bf16[8,256,384]{2,1,0:T(8,128)(2,1)} %bitcast.130), kind=kOutput, calls=%fused_computation.35 | convolution fusion | flops 1815869440 | bytes 10350592 | tf_op jit(solution)/shard_map/lse,de->lsd/dot_general | solution.py:31
  243.8 2.0 multiply_reduce_fusion.5
  246.6 3.0 multiply_reduce_fusion.4
  249.7 2.4 fusion.43
  252.2 7.1 %reduce-scatter.8.cloned.1.call-done = f32[96,1152]{1,0:T(8,128)} async-done(((f32[384,1152]{1,0:T(8,128)}), f32[96,1152]{1,0:T(8,128)}) %reduce-scatter.8.cloned.1.call-update) | async-done | bytes 442384 | tf_op jit(solution)/shard_map/reduce_scatter | solution.py:228
  259.3 49.4 %reduce-scatter.14.cloned.1.call-done = f32[384,384]{1,0:T(8,128)} async-done(((f32[1536,384]{1,0:T(8,128)}), f32[384,384]{1,0:T(8,128)}) %reduce-scatter.14.cloned.1.call-update) | async-done | bytes 589840 | tf_op jit(solution)/shard_map/reduce_scatter | solution.py:234
  308.8 50.0 %reduce-scatter.12.cloned.1.call-done = f32[96,1536]{1,0:T(8,128)} async-done(((f32[384,1536]{1,0:T(8,128)}), f32[96,1536]{1,0:T(8,128)}) %reduce-scatter.12.cloned.1.call-update) | async-done | bytes 589840 | tf_op jit(solution)/shard_map/reduce_scatter | solution.py:232
  358.7 68.3 %reduce-scatter.6.cloned.1.call-done = f32[96,2304]{1,0:T(8,128)} async-done(((f32[384,2304]{1,0:T(8,128)}), f32[96,2304]{1,0:T(8,128)}) %reduce-scatter.6.cloned.1.call-update) | async-done | bytes 884752 | tf_op jit(solution)/shard_map/reduce_scatter | solution.py:226
  430.4 18.0 %all-reduce.11 = (f32[2304]{0:T(1024)S(1)}, f32[768]{0:T(1024)S(1)}, f32[384]{0:T(512)S(1)}, f32[1536]{0:T(1024)S(1)}, f32[384]{0:T(512)S(1)}) all-reduce(f32[2304]{0:T(1024)S(1)} %convert_reduce_fusion.5, f32[768]{0:T(1024)S(1)} %pad_maximum_fusion, f32[384]{0:T(512)S(1)} %copy-done.45, ...), channel_id=3, replica_groups=mesh['shard'=4,'rep'=8] {'shard'}, use_global_device_ids=true, to_apply=%region_20.21.clone | all-reduce | flops 5376 | bytes 43008
  448.8 12.7 %all-reduce.9 = (f32[576]{0:T(1024)}, f32[192]{0:T(256)}, f32[96]{0:T(128)}, f32[384]{0:T(512)}, f32[96]{0:T(128)}) all-reduce(f32[576]{0:T(1024)S(1)} %dynamic-slice.5, f32[192]{0:T(256)S(1)} %dynamic-slice.7, f32[96]{0:T(128)S(1)} %dynamic-slice.9, f32[384]{0:T(512)S(1)} %dynamic-slice.11, ...), channel_id=1, replica_groups=mesh['shard'=4,'rep'=8] {'rep'}, use_global_device_ids=true, to_apply=%region_21.22 | all-reduce | flops 1344 | bytes 10752 | tf_op jit(solution)/shard_map/psum | solution.py:237
  461.5 1.2 fusion.38
  462.7 35.6 %all-reduce.15.cloned.1.call-done = (f32[96,2304]{1,0:T(8,128)}, f32[96,1152]{1,0:T(8,128)}, f32[96,384]{1,0:T(8,128)}, f32[96,1536]{1,0:T(8,128)}, f32[384,384]{1,0:T(8,128)}) async-done(((f32[96,2304]{1,0:T(8,128)}, f32[96,1152]{1,0:T(8,128)}, f32[96,384]{1,0:T(8,128)}, f32[96,1536]{1,0:T(8,128)}, f32[384,384]{1,0:T(8,128)}), (f32[96,2304]{1,0:T(8,128)}, f32[96,1152]{1,0:T(8,128)}, f32[96,384]{1,0:T(8,128)}, ...) | async-done | bytes 2654224 | tf_op jit(solution)/shard_map/psum | solution.py:237
  498.3 2.2 copy.114
  500.5 1.8 copy.115
  502.3 1.6 copy.116
  (188 shorter events, 15.7 us)
Async XLA Ops:
  7.2 5.0 copy-start.49
  7.2 4.2 copy-start.1
  7.2 7.5 %copy-start.51 = (bf16[384]{0:T(512)(128)(2,1)S(1)}, bf16[384]{0:T(512)(128)(2,1)}, u32[]{:S(2)}) copy-start(bf16[384]{0:T(512)(128)(2,1)} %param.22) | copy-start | bytes 2308
  7.2 21.9 %copy-start.54 = (bf16[96]{0:T(256)(128)(2,1)S(1)}, bf16[96]{0:T(256)(128)(2,1)}, u32[]{:S(2)}) copy-start(bf16[96]{0:T(256)(128)(2,1)} %param.24) | copy-start | bytes 580
  7.2 22.1 %copy-start.55 = (bf16[96]{0:T(256)(128)(2,1)S(1)}, bf16[96]{0:T(256)(128)(2,1)}, u32[]{:S(2)}) copy-start(bf16[96]{0:T(256)(128)(2,1)} %param.20) | copy-start | bytes 580
  7.2 22.3 %copy-start.56 = (bf16[192]{0:T(256)(128)(2,1)S(1)}, bf16[192]{0:T(256)(128)(2,1)}, u32[]{:S(2)}) copy-start(bf16[192]{0:T(256)(128)(2,1)} %param.18) | copy-start | bytes 1156
  7.2 22.6 %copy-start.50 = (bf16[576]{0:T(1024)(128)(2,1)S(1)}, bf16[576]{0:T(1024)(128)(2,1)}, u32[]{:S(2)}) copy-start(bf16[576]{0:T(1024)(128)(2,1)} %param.16) | copy-start | bytes 3460
  7.3 42.9 %copy-start.33 = (bf16[96,384]{1,0:T(8,128)(2,1)S(1)}, bf16[96,384]{1,0:T(8,128)(2,1)}, u32[]{:S(2)}) copy-start(bf16[96,384]{1,0:T(8,128)(2,1)} %param.19) | copy-start | bytes 221188
  7.3 57.8 %copy-start.20 = (bf16[96,1152]{1,0:T(8,128)(2,1)S(1)}, bf16[96,1152]{1,0:T(8,128)(2,1)}, u32[]{:S(2)}) copy-start(bf16[96,1152]{1,0:T(8,128)(2,1)} %param.17) | copy-start | bytes 663556
  7.3 85.9 %copy-start.34 = (bf16[8,384]{1,0:T(8,128)(2,1)S(1)}, bf16[8,384]{1,0:T(8,128)(2,1)}, u32[]{:S(2)}) copy-start(bf16[8,384]{1,0:T(8,128)(2,1)} %param.14) | copy-start | bytes 18436
  7.3 85.9 %all-gather.5.cloned.1.call-start = ((), (), s32[]{:S(2)}) async-start(), calls=%async_computation.5 | async-start | bytes 2211840 | tf_op jit(solution)/shard_map/all_gather | solution.py:74
  8.0 116.2 %all-gather.7.cloned.1.call-start = ((), (), s32[]{:S(2)}) async-start(), calls=%async_computation.6 | async-start | bytes 1474560 | tf_op jit(solution)/shard_map/all_gather | solution.py:80
  8.8 126.1 %all-gather.9.cloned.1.call-start = ((), (), s32[]{:S(2)}) async-start(), calls=%async_computation.7 | async-start | bytes 1474560 | tf_op jit(solution)/shard_map/all_gather | solution.py:82
  9.5 242.7 %reduce-scatter.10.cloned.1.call-start = ((), (), s32[]{:S(2)}) async-start(), calls=%async_computation.10 | async-start | bytes 737280 | tf_op jit(solution)/shard_map/reduce_scatter | solution.py:230
  11.4 89.4 %copy-start.25 = (f32[8,256]{1,0:T(8,128)}, f32[8,256]{1,0:T(8,128)S(1)}, u32[]{:S(2)}) copy-start(f32[8,256]{1,0:T(8,128)S(1)} %div.44) | copy-start | bytes 24580
  50.2 50.6 %copy-start.31 = (f32[8,256]{1,0:T(8,128)}, f32[8,256]{1,0:T(8,128)S(1)}, u32[]{:S(2)}) copy-start(f32[8,256]{1,0:T(8,128)S(1)} %add.168) | copy-start | bytes 24580
  50.2 50.6 %copy-start.27 = (f32[8,256]{1,0:T(8,128)}, f32[8,256]{1,0:T(8,128)S(1)}, u32[]{:S(2)}) copy-start(f32[8,256]{1,0:T(8,128)S(1)} %rsqrt.23) | copy-start | bytes 24580
  93.2 7.6 %copy-start.17 = (bf16[384,1152]{1,0:T(8,128)(2,1)}, bf16[384,1152]{1,0:T(8,128)(2,1)S(1)}, u32[]{:S(2)}) copy-start(bf16[384,1152]{1,0:T(8,128)(2,1)S(1)} %all_gather.37) | copy-start | bytes 2654212
  95.9 4.8 copy-start.21
  96.0 4.8 copy-start.38
  111.2 4.5 copy-start
  115.7 3.9 copy-start.2
  115.7 3.9 copy-start.23
  115.7 3.9 copy-start.43
  134.9 9.4 %copy-start.36 = (f32[8,384]{1,0:T(8,128)S(1)}, f32[8,384]{1,0:T(8,128)}, u32[]{:S(2)}) copy-start(f32[8,384]{1,0:T(8,128)} %get-tuple-element.48) | copy-start | bytes 36868
  134.9 9.4 %copy-start.47 = (f32[1536]{0:T(1024)S(1)}, f32[1536]{0:T(1024)}, u32[]{:S(2)}) copy-start(f32[1536]{0:T(1024)} %reshape.201) | copy-start | bytes 18436
  134.9 9.4 %copy-start.53 = (bf16[1536,384]{1,0:T(8,128)(2,1)S(1)}, bf16[1536,384]{1,0:T(8,128)(2,1)}, u32[]{:S(2)}) copy-start(bf16[1536,384]{1,0:T(8,128)(2,1)} %all-gather.9.cloned.1.call-done) | copy-start | bytes 3538948
  144.3 20.8 %copy-start.15 = (f32[2048,384]{1,0:T(8,128)}, f32[2048,384]{1,0:T(8,128)S(1)}, u32[]{:S(2)}) copy-start(f32[2048,384]{1,0:T(8,128)S(1)} %get-tuple-element.44) | copy-start | bytes 9437188
  144.3 14.6 %copy-start.52 = (bf16[384,1536]{1,0:T(8,128)(2,1)S(1)}, bf16[384,1536]{1,0:T(8,128)(2,1)}, u32[]{:S(2)}) copy-start(bf16[384,1536]{1,0:T(8,128)(2,1)} %all-gather.7.cloned.1.call-done) | copy-start | bytes 3538948
  158.9 3.8 copy-start.5
  158.9 3.8 copy-start.30
  165.0 4.7 copy-start.13
  177.8 8.6 %copy-start.6 = (bf16[8,256,384]{1,2,0:T(8,128)(2,1)S(1)}, bf16[8,256,384]{1,2,0:T(8,128)(2,1)}, u32[]{:S(2)}) copy-start(bf16[8,256,384]{1,2,0:T(8,128)(2,1)} %copy.77) | copy-start | bytes 4718596
  196.0 63.4 %reduce-scatter.8.cloned.1.call-start = ((), (), s32[]{:S(2)}) async-start(), calls=%async_computation.9 | async-start | bytes 2211840 | tf_op jit(solution)/shard_map/reduce_scatter | solution.py:228
  220.8 87.9 %reduce-scatter.14.cloned.1.call-start = ((), (), s32[]{:S(2)}) async-start(), calls=%async_computation.12 | async-start | bytes 2949120 | tf_op jit(solution)/shard_map/reduce_scatter | solution.py:234
  229.5 7.4 %copy-start.26 = (f32[8,256]{1,0:T(8,128)S(1)}, f32[8,256]{1,0:T(8,128)}, u32[]{:S(2)}) copy-start(f32[8,256]{1,0:T(8,128)} %copy-done.25) | copy-start | bytes 24580
  229.5 129.3 %reduce-scatter.12.cloned.1.call-start = ((), (), s32[]{:S(2)}) async-start(), calls=%async_computation.11 | async-start | bytes 2949120 | tf_op jit(solution)/shard_map/reduce_scatter | solution.py:232
  236.6 7.1 %copy-start.32 = (f32[8,256]{1,0:T(8,128)S(1)}, f32[8,256]{1,0:T(8,128)}, u32[]{:S(2)}) copy-start(f32[8,256]{1,0:T(8,128)} %copy-done.31) | copy-start | bytes 24580
  236.6 7.1 %copy-start.4 = (bf16[2048,384]{1,0:T(8,128)(2,1)S(1)}, bf16[2048,384]{1,0:T(8,128)(2,1)}, u32[]{:S(2)}) copy-start(bf16[2048,384]{1,0:T(8,128)(2,1)} %param.13) | copy-start | bytes 4718596
  236.6 7.1 %copy-start.28 = (f32[8,256]{1,0:T(8,128)S(1)}, f32[8,256]{1,0:T(8,128)}, u32[]{:S(2)}) copy-start(f32[8,256]{1,0:T(8,128)} %copy-done.27) | copy-start | bytes 24580
  236.6 190.4 %reduce-scatter.6.cloned.1.call-start = ((), (), s32[]{:S(2)}) async-start(), calls=%async_computation.8 | async-start | bytes 4423680 | tf_op jit(solution)/shard_map/reduce_scatter | solution.py:226
  252.1 177.5 %copy-start.16 = (bf16[2048,384]{1,0:T(8,128)(2,1)S(1)}, bf16[2048,384]{1,0:T(8,128)(2,1)}, u32[]{:S(2)}) copy-start(bf16[2048,384]{1,0:T(8,128)(2,1)} %param.25) | copy-start | bytes 4718596
  252.1 178.2 %copy-start.45 = (f32[384]{0:T(512)S(1)}, f32[384]{0:T(512)}, u32[]{:S(2)}) copy-start(f32[384]{0:T(512)} %get-tuple-element.38) | copy-start | bytes 4612
  252.1 178.2 %copy-start.46 = (f32[1536]{0:T(1024)S(1)}, f32[1536]{0:T(1024)}, u32[]{:S(2)}) copy-start(f32[1536]{0:T(1024)} %get-tuple-element.74) | copy-start | bytes 18436
  252.1 209.4 %copy-start.9 = (bf16[384,2304]{1,0:T(8,128)(2,1)S(1)}, bf16[384,2304]{1,0:T(8,128)(2,1)}, u32[]{:S(2)}) copy-start(bf16[384,2304]{1,0:T(8,128)(2,1)} %all-gather.5.cloned.1.call-done) | copy-start | bytes 5308420
  252.2 246.1 %all-reduce.15.cloned.1.call-start = ((), (), s32[]{:S(2)}) async-start(), calls=%async_computation.13 | async-start | bytes 5308416 | tf_op jit(solution)/shard_map/psum | solution.py:237
  498.3 5.6 %copy-start.19 = (f32[96,1536]{1,0:T(8,128)S(1)}, f32[96,1536]{1,0:T(8,128)}, u32[]{:S(2)}) copy-start(f32[96,1536]{1,0:T(8,128)} %get-tuple-element.85) | copy-start | bytes 1769476
  498.3 6.4 %copy-start.18 = (f32[384,384]{1,0:T(8,128)S(1)}, f32[384,384]{1,0:T(8,128)}, u32[]{:S(2)}) copy-start(f32[384,384]{1,0:T(8,128)} %get-tuple-element.87) | copy-start | bytes 1769476
  (18 other events, 45.4 us)
Sparse Core Ops, SparseCore 0:
  9.7 45.7 all-gather.4
  57.1 39.3 all-gather.6
  98.0 29.6 all-gather.8
  196.1 21.9 reduce-scatter.9
  220.9 38.3 reduce-scatter.7
  261.6 47.1 reduce-scatter.13
  311.2 47.5 reduce-scatter.11
  361.2 65.8 reduce-scatter.5
  431.5 66.7 all-reduce.14
where the time goes:
time: 516 us; the launch traced here: 512 us
  waiting for transfers between devices  213 us (41%)
  matrix products  115 us (22%)
  blocking collectives  106 us (21%)
  other arithmetic  31.7 us (6%)
  local copies, waits for them, and re-layouts  27.3 us (5%)
  between operations  19.4 us (4%)
    reduce_scatter x1, waiting for transfers between devices, shards(): lax.psum_scatter(partials[0], 'shard', scatter_dimension=0, tiled=True)  68.3 us
    reduce_scatter x1, waiting for transfers between devices, shards(): lax.psum_scatter(partials[6], 'shard', scatter_dimension=0, tiled=True)  50 us
    reduce_scatter x1, waiting for transfers between devices, shards(): lax.psum_scatter(partials[8], 'shard', scatter_dimension=0, tiled=True)  49.4 us
    unnamed x2, blocking collectives  36.3 us
    psum x1, waiting for transfers between devices, shards(): lax.psum((owned[0], owned[1], owned[2], owned[3], owned[4], owned[5], own...  35.6 us
    dot_general x4, matrix products, project_back(): jnp.einsum('lse,de->lsd', gradient, weight, preferred_element_type=jnp.fl...  28.7 us
    all_gather x1, blocking collectives, shards(): lax.all_gather(qkv_weight, 'shard', axis=0, tiled=True)  28.1 us
    dot_general x4, matrix products, project(): jnp.einsum('lsd,de->lse', inputs, weight, preferred_element_type=jnp.floa...  27.7 us
  transfers between devices with their start and end apart: 9, of which 5 were waited for; matrix products, arithmetic and copies ran while one was open for 19% of the time, Pallas kernels for 0%

commit v1 on v0

--- a/solution.py
+++ b/solution.py
@@ -37,6 +37,104 @@
 
 def column_sums(gradient):
     return jnp.sum(gradient, axis=(0, 1), dtype=jnp.float32)
+
+
+def rep_bits(rep_count):
+    return [1 << i for i in range(rep_count.bit_length() - 1)]
+
+
+def swap_rep(values, bit, rep_count):
+    return lax.ppermute(values, "rep", [(i, i ^ bit) for i in range(rep_count)])
+
+
+def to_shard(values, hop, shard_count):
+    return lax.ppermute(values, "shard", [(i, (i + hop) % shard_count) for i in range(shard_count)])
+
+
+def gather_near(values, shard_count):
+    return [values] + [
+        to_shard(values, shard_count - hop, shard_count) for hop in range(1, shard_count)
+    ]
+
+
+def in_order(pieces, shard_at):
+    count = len(pieces)
+    doubled = jnp.stack(pieces + pieces)
+    return lax.dynamic_slice_in_dim(doubled, count - shard_at, count, axis=0)
+
+
+def column_blocks(weight, width):
+    return jnp.concatenate(jnp.split(weight, weight.shape[1] // width, axis=1), axis=0)
+
+
+def unblock(rows, height):
+    return jnp.concatenate(jnp.split(rows, rows.shape[0] // height, axis=0), axis=1)
+
+
+def wide_matrix(blocks, columns):
+    count, rows, width = blocks.shape
+    groups = columns // width
+    return jnp.concatenate(
+        [
+            blocks[:, i * rows // groups : (i + 1) * rows // groups].reshape(-1, width)
+            for i in range(groups)
+        ],
+        axis=1,
+    )
+
+
+def block_grad(grad, shard_count):
+    rows, columns = grad.shape
+    pieces = jnp.split(grad, columns // rows, axis=1)
+    return jnp.concatenate([piece.reshape(shard_count, -1, rows) for piece in pieces], axis=1)
+
+
+def gather_shards(rows, shard_count, shard_at, rep_count, rep_at):
+    half = rows.shape[0] // 2
+    core = rep_at % 2
+    mine = lax.dynamic_slice_in_dim(rows, core * half, half, axis=0)
+    fetched = jnp.stack(gather_near(mine, shard_count)[1:])
+    other = swap_rep(fetched, 1, rep_count)
+    low_rows = jnp.where(core == 0, fetched, other)
+    high_rows = jnp.where(core == 0, other, fetched)
+    joined = jnp.concatenate([low_rows, high_rows], axis=1)
+    return in_order([rows] + [joined[i] for i in range(shard_count - 1)], shard_at)
+
+
+def reduce_rows(partial, shard_count, shard_at, rep_count, rep_at):
+    kept = partial
+    bits = rep_bits(rep_count)
+    for at, bit in enumerate(bits):
+        side = (rep_at >> at) & 1
+        half = kept.shape[1] // 2
+        sent = lax.dynamic_slice_in_dim(kept, (1 - side) * half, half, axis=1)
+        came = swap_rep(sent.astype(jnp.bfloat16), bit, rep_count)
+        kept = lax.dynamic_slice_in_dim(kept, side * half, half, axis=1) + came.astype(jnp.float32)
+    total = lax.dynamic_index_in_dim(kept, shard_at, 0, keepdims=False)
+    for hop in range(1, shard_count):
+        target = (shard_at + hop) % shard_count
+        sent = lax.dynamic_index_in_dim(kept, target, 0, keepdims=False)
+        came = to_shard(sent.astype(jnp.bfloat16), hop, shard_count)
+        total = total + came.astype(jnp.float32)
+    whole = total.astype(jnp.bfloat16)
+    for at in range(len(bits) - 1, -1, -1):
+        side = (rep_at >> at) & 1
+        other = swap_rep(whole, bits[at], rep_count)
+        whole = jnp.concatenate(
+            [jnp.where(side == 0, whole, other), jnp.where(side == 0, other, whole)], axis=0
+        )
+    return whole.astype(jnp.float32)
+
+
+def sum_small(partial, shard_count, shard_at, rep_count):
+    for bit in rep_bits(rep_count):
+        partial = partial + swap_rep(partial, bit, rep_count)
+    total = lax.dynamic_index_in_dim(partial, shard_at, 0, keepdims=False)
+    for hop in range(1, shard_count):
+        target = (shard_at + hop) % shard_count
+        sent = lax.dynamic_index_in_dim(partial, target, 0, keepdims=False)
+        total = total + to_shard(sent, hop, shard_count)
+    return total
 
 
 def shards(
@@ -59,35 +157,46 @@
     seq_length = latents_in.shape[0] // latent_count
     head_count = model_width // HEAD_DIM
     softmax_scale = HEAD_DIM ** (-0.5)
-    (
-        mod_weight,
-        mod_bias,
-        qkv_matrix,
-        qv_offsets,
-        proj_matrix,
-        proj_offsets,
-        up_matrix,
-        up_offsets,
-        down_matrix,
-        down_offsets,
-    ) = (
-        lax.all_gather(ada_weight, "shard", axis=0, tiled=True),
-        lax.all_gather(ada_bias, "shard", axis=0, tiled=True),
-        lax.all_gather(qkv_weight, "shard", axis=0, tiled=True),
-        lax.all_gather(qv_bias, "shard", axis=0, tiled=True),
-        lax.all_gather(proj_weight, "shard", axis=0, tiled=True),
-        lax.all_gather(proj_bias, "shard", axis=0, tiled=True),
-        lax.all_gather(fc1_weight, "shard", axis=0, tiled=True),
-        lax.all_gather(fc1_bias, "shard", axis=0, tiled=True),
-        lax.all_gather(fc2_weight, "shard", axis=0, tiled=True),
-        lax.all_gather(fc2_bias, "shard", axis=0, tiled=True),
-    )
+    shard_count = lax.axis_size("shard")
+    rep_count = lax.axis_size("rep")
+    shard_at = lax.axis_index("shard")
+    rep_at = lax.axis_index("rep")
+    part = model_width // shard_count
+    small_rows = jnp.concatenate([qv_bias, proj_bias, fc1_bias, fc2_bias])
+    small_rows = small_rows.reshape(-1, model_width)
+    first_pack = gather_near(jnp.concatenate([conditioning, small_rows], axis=0), shard_count)
+    cond_near = jnp.concatenate([piece[:latent_count] for piece in first_pack], axis=0)
+    qkv_blocks = gather_shards(column_blocks(qkv_weight, model_width), shard_count, shard_at, rep_count, rep_at)
+    late_blocks = gather_shards(
+        jnp.concatenate([proj_weight, column_blocks(fc1_weight, model_width), fc2_weight], axis=0),
+        shard_count, shard_at, rep_count, rep_at,
+    )
+    silu_near = jax.nn.silu(cond_near.astype(jnp.float32)).astype(jnp.bfloat16)
+    silu_mine = lax.dynamic_slice_in_dim(silu_near, shard_at * part, part, axis=1)
+    mod_part = jnp.dot(silu_mine, ada_weight, preferred_element_type=jnp.float32)
+    wide_bias = lax.dynamic_update_slice_in_dim(
+        jnp.zeros((ada_weight.shape[1],), jnp.float32), ada_bias.astype(jnp.float32),
+        shard_at * ada_bias.shape[0], axis=0,
+    )
+    mod_part = (mod_part + wide_bias).reshape(shard_count, latent_count, -1)
+    modulation = mod_part[0]
+    for hop in range(1, shard_count):
+        modulation = modulation + to_shard(mod_part[hop], hop, shard_count)
+    small_all = in_order([piece[latent_count:] for piece in first_pack], shard_at)
+    small_all = small_all.reshape(shard_count, -1)
+    edges = [0]
+    for vector in (qv_bias, proj_bias, fc1_bias, fc2_bias):
+        edges.append(edges[-1] + vector.shape[0])
+    qv_offsets, proj_offsets, up_offsets, down_offsets = (
+        small_all[:, edges[i] : edges[i + 1]].reshape(-1) for i in range(4)
+    )
+    qkv_matrix = wide_matrix(qkv_blocks, qkv_weight.shape[1])
+    proj_matrix = late_blocks[:, :part].reshape(model_width, model_width)
+    up_rows = part * (fc1_weight.shape[1] // model_width)
+    up_matrix = wide_matrix(late_blocks[:, part : part + up_rows], fc1_weight.shape[1])
+    down_matrix = late_blocks[:, part + up_rows :].reshape(-1, model_width)
     inputs = latents_in.astype(jnp.float32).reshape(latent_count, seq_length, model_width)
-    cond_silu, silu_pull = jax.vjp(jax.nn.silu, conditioning.astype(jnp.float32))
-    silu_low = cond_silu.astype(jnp.bfloat16)
-    modulation = jnp.dot(
-        silu_low, mod_weight, preferred_element_type=jnp.float32
-    ) + mod_bias.astype(jnp.float32)
+    _, silu_pull = jax.vjp(jax.nn.silu, conditioning.astype(jnp.float32))
     shift_one, scale_one, gate_one, shift_two, scale_two, gate_two = jnp.split(
         modulation, 6, axis=1
     )
@@ -122,29 +231,6 @@
     hidden_low = hidden_act.astype(jnp.bfloat16)
     branch_out = project(hidden_low, down_matrix) + down_offsets.astype(jnp.float32)
     result = middle + gate_two[:, None, :] * branch_out
-    (
-        mod_weight,
-        mod_bias,
-        qkv_matrix,
-        qv_offsets,
-        proj_matrix,
-        proj_offsets,
-        up_matrix,
-        up_offsets,
-        down_matrix,
-        down_offsets,
-    ) = (
-        lax.all_gather(ada_weight, "shard", axis=0, tiled=True),
-        lax.all_gather(ada_bias, "shard", axis=0, tiled=True),
-        lax.all_gather(qkv_weight, "shard", axis=0, tiled=True),
-        lax.all_gather(qv_bias, "shard", axis=0, tiled=True),
-        lax.all_gather(proj_weight, "shard", axis=0, tiled=True),
-        lax.all_gather(proj_bias, "shard", axis=0, tiled=True),
-        lax.all_gather(fc1_weight, "shard", axis=0, tiled=True),
-        lax.all_gather(fc1_bias, "shard", axis=0, tiled=True),
-        lax.all_gather(fc2_weight, "shard", axis=0, tiled=True),
-        lax.all_gather(fc2_bias, "shard", axis=0, tiled=True),
-    )
     upstream = cotangent.astype(jnp.float32).reshape(latent_count, seq_length, model_width)
     down_grad = (gate_two[:, None, :] * upstream).astype(jnp.bfloat16)
     gate_two_grad = jnp.sum(upstream * branch_out, axis=1)
@@ -153,6 +239,14 @@
     hidden_grad = gelu_pull(project_back(down_grad, down_matrix))[0].astype(jnp.bfloat16)
     up_w_grad = weight_grad(second_low, hidden_grad)
     up_b_grad = column_sums(hidden_grad)
+    early = jnp.concatenate(
+        [
+            down_w_grad.reshape(shard_count, -1, model_width),
+            block_grad(up_w_grad, shard_count),
+        ],
+        axis=1,
+    )
+    early_sum = reduce_rows(early, shard_count, shard_at, rep_count, rep_at)
     middle_part, shift_two_grad, scale_two_grad = second_pull(project_back(hidden_grad, up_matrix))
     middle_grad = upstream + middle_part
     attn_grad = (gate_one[:, None, :] * middle_grad).astype(jnp.bfloat16)
@@ -205,62 +299,48 @@
         ],
         axis=1,
     ).astype(jnp.bfloat16)
-    ada_w_grad = jnp.einsum("ld,le->de", silu_low, mod_grad, preferred_element_type=jnp.float32)
-    ada_b_grad = jnp.sum(mod_grad, axis=0, dtype=jnp.float32)
-    cond_grad = silu_pull(
-        jnp.einsum("le,de->ld", mod_grad, mod_weight, preferred_element_type=jnp.float32)
-    )[0]
-    partials = (
-        ada_w_grad,
-        ada_b_grad,
-        qkv_w_grad,
-        qv_b_grad,
-        proj_w_grad,
-        proj_b_grad,
-        up_w_grad,
-        up_b_grad,
-        down_w_grad,
-        down_b_grad,
-    )
-    owned = (
-        lax.psum_scatter(partials[0], "shard", scatter_dimension=0, tiled=True),
-        lax.psum_scatter(partials[1], "shard", scatter_dimension=0, tiled=True),
-        lax.psum_scatter(partials[2], "shard", scatter_dimension=0, tiled=True),
-        lax.psum_scatter(partials[3], "shard", scatter_dimension=0, tiled=True),
-        lax.psum_scatter(partials[4], "shard", scatter_dimension=0, tiled=True),
-        lax.psum_scatter(partials[5], "shard", scatter_dimension=0, tiled=True),
-        lax.psum_scatter(partials[6], "shard", scatter_dimension=0, tiled=True),
-        lax.psum_scatter(partials[7], "shard", scatter_dimension=0, tiled=True),
-        lax.psum_scatter(partials[8], "shard", scatter_dimension=0, tiled=True),
-        lax.psum_scatter(partials[9], "shard", scatter_dimension=0, tiled=True),
-    )
-    finals = lax.psum(
-        (
-            owned[0],
-            owned[1],
-            owned[2],
-            owned[3],
-            owned[4],
-            owned[5],
-            owned[6],
-            owned[7],
-            owned[8],
-            owned[9],
-        ),
-        "rep",
-    )
-    (
-        final_ada_w,
-        final_ada_b,
-        final_qkv_w,
-        final_qv_b,
-        final_proj_w,
-        final_proj_b,
-        final_up_w,
-        final_up_b,
-        final_down_w,
-        final_down_b,
-    ) = finals
+    late = jnp.concatenate(
+        [proj_w_grad.reshape(shard_count, -1, model_width), block_grad(qkv_w_grad, shard_count)],
+        axis=1,
+    )
+    late_sum = reduce_rows(late, shard_count, shard_at, rep_count, rep_at)
+    small_grads = jnp.concatenate(
+        [
+            vector.reshape(shard_count, -1)
+            for vector in (qv_b_grad, proj_b_grad, up_b_grad, down_b_grad)
+        ],
+        axis=1,
+    )
+    small_final = sum_small(small_grads, shard_count, shard_at, rep_count)
+    mod_near = jnp.concatenate(gather_near(mod_grad, shard_count), axis=0)
+    cond_part = jnp.einsum("le,de->ld", mod_near, ada_weight, preferred_element_type=jnp.float32)
+    cond_part = cond_part.reshape(shard_count, latent_count, part)
+    pieces = [cond_part[0]]
+    for hop in range(1, shard_count):
+        pieces.append(to_shard(cond_part[hop], hop, shard_count))
+    pieces = pieces[:1] + pieces[:0:-1]
+    cond_grad = in_order(pieces, shard_at)
+    cond_grad = cond_grad.transpose(1, 0, 2).reshape(latent_count, model_width)
+    cond_grad = silu_pull(cond_grad)[0]
+    mod_all, silu_all = mod_near, silu_mine
+    for bit in rep_bits(rep_count)[::-1]:
+        mod_all = jnp.concatenate([mod_all, swap_rep(mod_all, bit, rep_count)], axis=0)
+        silu_all = jnp.concatenate([silu_all, swap_rep(silu_all, bit, rep_count)], axis=0)
+    final_ada_w = jnp.einsum("ld,le->de", silu_all, mod_all, preferred_element_type=jnp.float32)
+    bias_cols = ada_bias.shape[0]
+    final_ada_b = jnp.sum(
+        lax.dynamic_slice_in_dim(mod_all, shard_at * bias_cols, bias_cols, axis=1),
+        axis=0,
+        dtype=jnp.float32,
+    )
+    down_rows = fc2_weight.shape[0]
+    final_down_w = early_sum[:down_rows]
+    final_up_w = unblock(early_sum[down_rows:], part)
+    final_proj_w = late_sum[:part]
+    final_qkv_w = unblock(late_sum[part:], part)
+    final_qv_b, final_proj_b, final_up_b, final_down_b = (
+        small_final[edges[i] : edges[i + 1]] for i in range(4)
+    )
     return (
         result.reshape(latent_count * seq_length, model_width).astype(jnp.bfloat16),
         input_grad.reshape(latent_count * seq_length, model_width),

time: 516 us -> 344 us (0.67)
  waiting for transfers between devices: 213 us -> 50.1 us
  blocking collectives: 106 us -> 0 us
  starting transfers between devices: 0.57 us -> 61.9 us
  other arithmetic: 31.7 us -> 62.7 us
  local copies, waits for them, and re-layouts: 27.3 us -> 56.8 us
  between operations: 19.4 us -> 2.22 us
  matrix products: 115 us -> 105 us
    reduce_scatter x5 -> x0, waiting for transfers between devices: 175 us -> none  [the longest x1 68.3 us: shards(): lax.psum_scatter(partials[0], 'shard', scatter_dimension=0, tiled=True)]
    ppermute x0 -> x50, starting transfers between devices: none -> 61.9 us  [the longest x27 43.3 us: to_shard(): lax.ppermute(values, 'shard', [(i, (i + hop) % shard_count) for i in rang...]
    all_gather x3 -> x0, blocking collectives: 56.7 us -> none  [the longest x1 28.1 us: shards(): lax.all_gather(qkv_weight, 'shard', axis=0, tiled=True)]
    ppermute x0 -> x50, waiting for transfers between devices: none -> 50.1 us  [the longest x23 30.1 us: swap_rep(): return lax.ppermute(values, 'rep', [(i, i ^ bit) for i in range(rep_count)])]
    unnamed x2 -> x0, blocking collectives: 36.3 us -> none
    psum x1 -> x0, waiting for transfers between devices: 35.6 us -> none  [shards(): lax.psum((owned[0], owned[1], owned[2], owned[3], owned[4], owned[5], own...]
    psum x1 -> x0, blocking collectives: 12.7 us -> none  [shards(): lax.psum((owned[0], owned[1], owned[2], owned[3], owned[4], owned[5], own...]
    another operation x0 -> x4, other arithmetic: none -> 12.1 us  [the longest x2 8.35 us: in_order(): doubled = jnp.stack(pieces + pieces)]
  transfers between devices with their start and end apart: 9 -> 50, of which waited for: 5 -> 16; matrix products, arithmetic and copies ran while one was open for 19% -> 27% of each run, Pallas kernels for 0% -> 0%
where the time goes in v1:
time: 344 us; the launch traced here: 339 us
  matrix products  105 us (31%)
  other arithmetic  62.7 us (18%)
  starting transfers between devices  61.9 us (18%)
  local copies, waits for them, and re-layouts  56.8 us (17%)
  waiting for transfers between devices  50.1 us (15%)
    ppermute x27, starting transfers between devices, to_shard(): lax.ppermute(values, 'shard', [(i, (i + hop) % shard_count) for i in rang...  43.3 us
    ppermute x23, waiting for transfers between devices, swap_rep(): return lax.ppermute(values, 'rep', [(i, i ^ bit) for i in range(rep_count)])  30.1 us
    dot_general x4, matrix products, project(): jnp.einsum('lsd,de->lse', inputs, weight, preferred_element_type=jnp.floa...  30 us
    dot_general x4, matrix products, project_back(): jnp.einsum('lse,de->lsd', gradient, weight, preferred_element_type=jnp.fl...  22.8 us
    ppermute x27, waiting for transfers between devices, to_shard(): lax.ppermute(values, 'shard', [(i, (i + hop) % shard_count) for i in rang...  20 us
    ppermute x23, starting transfers between devices, swap_rep(): return lax.ppermute(values, 'rep', [(i, i ^ bit) for i in range(rep_count)])  18.6 us
    unnamed x174, local copies, waits for them, and re-layouts  17.6 us
    dot_general x4, matrix products, weight_grad(): jnp.einsum('lsd,lse->de', inputs, gradient, preferred_element_type=jnp.fl...  17.3 us
  transfers between devices with their start and end apart: 50, of which 16 were waited for; matrix products, arithmetic and copies ran while one was open for 27% of the time, Pallas kernels for 0%

profile of v1, /device:TPU:0, one launch (start us, length us, event | category | flops | bytes accessed | tf_op | source)
XLA Modules:
  0.0 339.0 jit_solution(15094961944636610064)
XLA Ops:
  2.4 3.0 collective-permute-start.2
  5.4 2.6 collective-permute-start.1
  21.3 3.4 collective-permute-start.3
  30.6 2.9 collective-permute-start.6
  33.6 4.2 %collective-permute-done.4 = f32[8,2304]{1,0:T(8,128)S(1)} collective-permute-done((f32[8,2304]{1,0:T(8,128)S(1)}, f32[8,2304]{1,0:T(8,128)S(1)}, u32[]{:S(2)}, u32[]{:S(2)}) %collective-permute-start.4) | collective-permute-done | bytes 73760 | tf_op jit(solution)/shard_map/ppermute | solution.py:51
  39.9 2.1 collective-permute-done.6
  45.0 3.0 convert_reduce_fusion.2
  50.7 8.8 %collective-permute-done.11 = bf16[432,384]{1,0:T(8,128)(2,1)S(1)} collective-permute-done((bf16[432,384]{1,0:T(8,128)(2,1)}, bf16[432,384]{1,0:T(8,128)(2,1)S(1)}, u32[]{:S(2)}, u32[]{:S(2)}) %collective-permute-start.11) | collective-permute-done | bytes 331808 | tf_op jit(solution)/shard_map/ppermute | solution.py:51
  65.6 4.6 %add_convert_fusion = bf16[8,256,1152]{2,1,0:T(8,128)(2,1)} fusion(f32[1152]{0:T(1024)S(1)} %copy-done.59, f32[8,384]{1,0:T(8,128)S(1)} %get-tuple-element.94, f32[8,384]{1,0:T(8,128)S(1)} %get-tuple-element.95, f32[8,256]{1,0:T(8,128)S(1)} %rsqrt.23, f32[8,256]{1,0:T(8,128)S(1)} %div.48, bf16[384,384]{1,0:T(8,128)(2,1)S(1)} %bitcast.285, ...), kind=kOutput, calls=%fused_computation.27 | convolution fusion | flops 1824030720 | bytes 7221760 | tf_op jit(solution)/shard_map/lsd,de->lse/dot_general | solution.py:27
  70.2 6.7 %copy.98 = bf16[8,256,1152]{1,2,0:T(8,128)(2,1)} copy(bf16[8,256,1152]{2,1,0:T(8,128)(2,1)} %add_convert_fusion) | data formatting | bytes 9437184 | tf_op jit(solution)/shard_map/convert_element_type | solution.py:209
  76.8 3.7 %multiply_reduce_fusion.1 = (f32[8,6,256]{2,1,0:T(8,128)S(1)}, f32[8,6,256,256]{2,3,1,0:T(8,128)S(1)}) fusion(bf16[8,256,3,6,64]{1,4,3,2,0:T(8,128)(2,1)} %bitcast.236), kind=kOutput, calls=%fused_computation.24 | convolution fusion | flops 408932352 | bytes 15777792 | tf_op jit(solution)/shard_map/lqhd,lkhd->lhqk/dot_general | solution.py:215
  80.6 2.6 exponential_reduce_fusion
  85.2 3.8 %convolution_convert_fusion.1 = bf16[8,6,64,256]{3,2,1,0:T(8,128)(2,1)S(1)} fusion(bf16[8,256,3,6,64]{1,4,3,2,0:T(8,128)(2,1)} %bitcast.237, f32[8,6,256,256]{2,3,1,0:T(8,128)S(1)} %get-tuple-element.123, f32[8,6,256]{2,1,0:T(8,128)S(1)} %log_add_fusion), kind=kOutput, calls=%fused_computation.86 | convolution fusion | flops 412876800 | bytes 15777792 | tf_op jit(solution)/shard_map/lhqk,lkhd->lqhd/dot_general | solution.py:221
  91.1 6.5 %fusion.24 = bf16[4,864,384]{2,1,0:T(8,128)(2,1)S(1)} fusion(s32[]{:T(128)S(6)} %select_n.210, bf16[1,864,384]{2,1,0:T(8,128)(2,1)S(1)} %bitcast.259, bf16[3,432,384]{2,1,0:T(8,128)(2,1)S(1)} %get-tuple-element.48, bf16[3,432,384]{2,1,0:T(8,128)(2,1)S(1)} %get-tuple-element.47), kind=kLoop, calls=%fused_computation.70 | loop fusion | flops 15925248 | bytes 5308420 | tf_op jit(solution)/shard_map/stack | solution.py:62
  99.6 3.9 %multiply_add_fusion = (f32[8,256,384]{2,1,0:T(8,128)}, f32[8,256,384]{2,1,0:T(8,128)}) fusion(f32[384]{0:T(512)S(1)} %reshape.344, f32[8,384]{1,0:T(8,128)S(1)} %copy-done.39, bf16[2048,384]{1,0:T(8,128)(2,1)S(1)} %copy-done.3, bf16[8,256,384]{1,2,0:T(8,128)(2,1)S(1)} %bitcast.245, bf16[384,384,1]{1,0,2:T(8,128)(2,1)S(1)} %bitcast.250), kind=kOutput, calls=%fused_computation.63 | convolution fusion | flops 607125504 | bytes 9745920 | tf_op jit(solution)/shard_map/lsd,de->lse/dot_general | solution.py:27
  103.5 2.2 reduce_sum.189
  105.8 2.7 multiply_reduce_fusion.8
  108.6 10.4 %fusion.14 = (bf16[1536,8,256]{0,2,1:T(8,128)(2,1)}, f32[8,256,1536]{2,1,0:T(8,128)}) fusion(f32[1536]{0:T(1024)S(1)} %copy-done.57, bf16[384,384]{1,0:T(8,128)(2,1)S(1)} %bitcast.275, bf16[384,384]{1,0:T(8,128)(2,1)S(1)} %bitcast.277, bf16[384,384]{1,0:T(8,128)(2,1)} %bitcast.279, bf16[384,384]{1,0:T(8,128)(2,1)S(1)} %bitcast.273, ...), kind=kOutput, calls=%fused_computation.17 | convolution fusion | flops 2456027136 | bytes 23246848 | tf_op jit(solution)/shard_map/lsd,de->lse/dot_general | solution.py:27
  119.0 13.1 %convert_reduce_fusion = (f32[1536]{0:T(1024)}, bf16[8,256,1536]{2,1,0:T(8,128)(2,1)S(1)}) fusion(f32[8,256,1536]{2,1,0:T(8,128)} %get-tuple-element.135, f32[1536]{0:T(1024)S(1)} %copy-done.57, bf16[8,256,384]{2,1,0:T(8,128)(2,1)S(1)} %bitcast.262, bf16[1536,384,1]{1,0,2:T(8,128)(2,1)S(1)} %bitcast.267), kind=kOutput, calls=%fused_computation.18 | convolution fusion | flops 2488269312 | bytes 21639168 | tf_op jit(solution)/shard_map/lse,de->lsd/dot_general | solution.py:31
  132.2 3.7 %multiply_reduce_fusion.7 = (f32[8,256]{1,0:T(8,128)S(1)}, f32[8,256,384]{2,1,0:T(8,128)S(1)}) fusion(f32[8,256,384]{2,1,0:T(8,128)S(1)} %copy-done.2, f32[8,384]{1,0:T(8,128)S(1)} %get-tuple-element.93, f32[8,256]{1,0:T(8,128)S(1)} %broadcast_multiply_fusion, bf16[8,256,1536]{2,1,0:T(8,128)(2,1)S(1)} %get-tuple-element.133, ...), kind=kOutput, calls=%fused_computation.59 | convolution fusion | flops 2423781376 | bytes 13791232 | tf_op jit(solution)/shard_map/lse,de->lsd/dot_general | solution.py:31
  135.9 4.3 %convolution_bitcast_fusion = f32[384,1536]{1,0:T(8,128)} fusion(bf16[8,256,1536]{2,1,0:T(8,128)(2,1)S(1)} %get-tuple-element.133, f32[8,256,384]{2,1,0:T(8,128)S(1)} %copy-done.2, f32[8,384]{1,0:T(8,128)S(1)} %get-tuple-element.92, f32[8,384]{1,0:T(8,128)S(1)} %get-tuple-element.93, f32[8,256]{1,0:T(8,128)S(1)} %fusion.80, ...), kind=kOutput, calls=%fused_computation.66 | convolution fusion | flops 2419851264 | bytes 11837440 | tf_op jit(solution)/shard_map/lsd,lse->de/dot_general | solution.py:35
  140.3 11.1 %multiply_reduce_fusion.2 = (bf16[8,384]{1,0:T(8,128)(2,1)}, f32[2048,384]{1,0:T(8,128)S(1)}, bf16[8,256,384]{2,1,0:T(8,128)(2,1)}, bf16[8,384]{1,0:T(8,128)(2,1...) fusion(f32[384]{0:T(512)S(1)} %copy-done.64, bf16[2048,384]{1,0:T(8,128)(2,1)S(1)} %copy-done.20, ...), kind=kOutput, calls=%fused_computation.49 | convolution fusion | flops 2461520896 | bytes 26428928 | tf_op jit(solution)/shard_map/lsd,de->lse/dot_general | solution.py:27
  151.4 2.9 convert_reduce_fusion.3
  155.4 2.3 convolution_convert_fusion
  157.8 2.8 copy.104
  160.6 8.7 %convolution_bitcast_fusion.2 = bf16[8,256,1,6,64]{1,4,3,0,2:T(8,128)(2,1)} fusion(bf16[8,256,6,64]{1,3,2,0:T(8,128)(2,1)} %bitcast.243, f32[8,6,256,256]{2,3,1,0:T(8,128)} %copy-done.1, f32[8,6,256]{2,1,0:T(8,128)S(1)} %log_add_fusion), kind=kOutput, calls=%fused_computation.78 | convolution fusion | flops 412090368 | bytes 15777792 | tf_op jit(solution)/shard_map/lhqk,lqhd->lkhd/dot_general | solution.py:263
  169.3 13.9 %multiply_reduce_fusion = (f32[8,6,256]{2,1,0:T(8,128)}, f32[8,6,256,256]{2,3,1,0:T(8,128)}) fusion(f32[8,6,256,256]{2,3,1,0:T(8,128)} %copy-done.1, f32[8,6,256]{2,1,0:T(8,128)S(1)} %log_add_fusion, bf16[8,256,6,64]{1,3,2,0:T(8,128)(2,1)} %bitcast.244, bf16[8,256,3,6,64]{1,4,3,2,0:T(8,128)(2,1)} %bitcast.238), kind=kOutput, calls=%fused_computation.20 | convolution fusion | flops 415223808 | bytes 28409856 | tf_op jit(solution)/shard_map/lqhd,lkhd->lhqk/dot_general | solution.py:269
  183.2 7.1 %multiply_convert_fusion = bf16[8,6,256,256]{2,3,1,0:T(8,128)(2,1)S(1)} fusion(f32[8,6,256,256]{2,3,1,0:T(8,128)} %get-tuple-element.129, f32[8,6,256,256]{2,3,1,0:T(8,128)S(1)} %bitcast.232, f32[8,6,256]{2,1,0:T(8,128)} %get-tuple-element.128, f32[8,6,256]{2,1,0:T(8,128)S(1)} %log_add_fusion), kind=kLoop, calls=%fused_computation.19 | loop fusion | flops 15728640 | bytes 31555584 | tf_op jit(solution)/shard_map/convert_element_type | solution.py:275
  196.3 3.6 %multiply_reduce_fusion.6 = (f32[8,256]{1,0:T(8,128)S(1)}, f32[8,256,384]{2,1,0:T(8,128)S(1)}) fusion(f32[8,384]{1,0:T(8,128)S(1)} %get-tuple-element.95, f32[8,256]{1,0:T(8,128)S(1)} %copy-done.41, bf16[8,256,1152]{1,2,0:T(8,128)(2,1)S(1)} %bitcast.247, bf16[384,384]{1,0:T(8,128)(2,1)S(1)} %bitcast.286, bf16[384,384]{1,0:T(8,128)(2,1)S(1)} %bitcast.284, ...), kind=kOutput, calls=%fused_computation.54 | convolution fusion | flops 1818523648 | bytes 10350592 | tf_op jit(solution)/shard_map/lse,de->lsd/dot_general | solution.py:31
  202.8 3.0 multiply_reduce_fusion.4
  208.7 5.7 %collective-permute-start.16 = (bf16[8,2304]{1,0:T(8,128)(2,1)S(1)}, bf16[8,2304]{1,0:T(8,128)(2,1)S(1)}, u32[]{:S(2)}, u32[]{:S(2)}) collective-permute-start(bf16[8,2304]{1,0:T(8,128)(2,1)S(1)} %get-tuple-element.105), channel_id=1, source_target_pairs={{0,8},{8,16},{16,24},{24,0},{1,9},{9,17},{17,25},{25,1},{2,10},{10... | collective-permute-start | bytes 110600 | tf_op jit(solution)/shard_map/ppermute | solution.py:51
  216.8 2.9 fusion.102
  221.7 6.1 %bitcast_dynamic-update-slice_fusion = f32[4,768,384]{2,1,0:T(8,128)S(1)} fusion(bf16[8,256,384,1]{2,1,0,3:T(8,128)(2,1)} %bitcast.261, bf16[8,32,4,8,384]{4,3,2,1,0:T(8,128)(2,1)} %bitcast.290), kind=kOutput, calls=%fused_computation.74 | convolution fusion | flops 2415919104 | bytes 10223616 | tf_op jit(solution)/shard_map/lsd,lse->de/dot_general | solution.py:35
  228.0 2.2 copy-done.16
  232.2 5.0 %convolution_bitcast_fusion.1 = f32[384,1152]{1,0:T(8,128)S(1)} fusion(bf16[8,256,384]{2,1,0:T(8,128)(2,1)} %bitcast.260, bf16[8,256,1152]{1,2,0:T(8,128)(2,1)} %bitcast.248), kind=kOutput, calls=%fused_computation.67 | convolution fusion | flops 1811939328 | bytes 8060928 | tf_op jit(solution)/shard_map/lsd,lse->de/dot_general | solution.py:35
  245.0 4.0 %collective-permute-start.40 = (f32[768]{0:T(1024)S(1)}, f32[768]{0:T(1024)S(1)}, u32[]{:S(2)}, u32[]{:S(2)}) collective-permute-start(f32[768]{0:T(1024)S(1)} %get-tuple-element.20), channel_id=1, source_target_pairs={{0,24},{8,0},{16,8},{24,16},{1,25},{9,1},{17,9},{25,17},{2,26},{10... | collective-permute-start | bytes 9224 | tf_op jit(solution)/shard_map/ppermute | solution.py:51
  253.0 2.2 collective-permute-start.18
  255.2 2.8 collective-permute-start.17
  267.2 4.9 %collective-permute-done.27 = bf16[4,96,384]{2,1,0:T(8,128)(2,1)S(1)} collective-permute-done((bf16[4,96,384]{2,1,0:T(8,128)(2,1)S(1)}, bf16[4,96,384]{2,1,0:T(8,128)(2,1)S(1)}, u32[]{:S(2)}, u32[]{:S(2)}) %collective-permute-start.27) | collective-permute-done | bytes 294944 | tf_op jit(solution)/shard_map/ppermute | solution.py:47
  277.4 4.0 %concatenate.123 = bf16[128,2304]{0,1:T(8,128)(2,1)} concatenate(bf16[8,2304]{0,1:T(8,128)(2,1)S(1)} %copy.117, bf16[8,2304]{0,1:T(8,128)(2,1)S(1)} %copy.118, bf16[8,2304]{0,1:T(8,128)(2,1)S(1)} %copy.119, bf16[8,2304]{0,1:T(8,128)(2,1)S(1)} %copy.120, bf16[32,2304]{0,1:T(8,128)(2,1)} %copy.121, bf16[64,2304]{0,1:T(8,128)(2,1)} %copy.122), dimensions={0} | concatenate | bytes 1179648 | tf_op jit(solution)/shard_map/concatenate | solution.py:327
  282.9 3.4 %collective-permute-start.31 = (bf16[48,384]{1,0:T(8,128)(2,1)S(1)}, bf16[48,384]{1,0:T(8,128)(2,1)S(1)}, u32[]{:S(2)}, u32[]{:S(2)}) collective-permute-start(bf16[48,384]{1,0:T(8,128)(2,1)S(1)} %get-tuple-element.75), channel_id=1, source_target_pairs={{0,24},{8,0},{16,8},{24,16},{1,25},{9,1},{17,9},{25,17},{2,26},{10... | collective-permute-start | bytes 110600 | tf_op jit(solution)/shard_map/ppermute | solution.py:51
  286.5 2.2 convert_add_fusion
  294.3 4.2 %concatenate.124 = bf16[256,2304]{0,1:T(8,128)(2,1)S(1)} concatenate(bf16[8,2304]{0,1:T(8,128)(2,1)S(1)} %copy.117, bf16[8,2304]{0,1:T(8,128)(2,1)S(1)} %copy.118, bf16[8,2304]{0,1:T(8,128)(2,1)} %copy-done.13, bf16[8,2304]{0,1:T(8,128)(2,1)} %copy-done.14, bf16[32,2304]{0,1:T(8,128)(2,1)} %copy.121, bf16[64,2304]{0,1:T(8,128)(2,1)} %copy.122, ...), dimensions={0} | concatenate | bytes 2359296 | tf_op jit(solution)/shard_map/concatenate | solution.py:327
  300.8 5.8 %collective-permute-done.42 = bf16[4,192,384]{2,1,0:T(8,128)(2,1)} collective-permute-done((bf16[4,192,384]{2,1,0:T(8,128)(2,1)}, bf16[4,192,384]{2,1,0:T(8,128)(2,1)}, u32[]{:S(2)}, u32[]{:S(2)}) %collective-permute-start.42) | collective-permute-done | bytes 589856 | tf_op jit(solution)/shard_map/ppermute | solution.py:47
  310.8 5.4 %collective-permute-done.43 = bf16[4,96,384]{2,1,0:T(8,128)(2,1)S(1)} collective-permute-done((bf16[4,96,384]{2,1,0:T(8,128)(2,1)S(1)}, bf16[4,96,384]{2,1,0:T(8,128)(2,1)S(1)}, u32[]{:S(2)}, u32[]{:S(2)}) %collective-permute-start.43) | collective-permute-done | bytes 294944 | tf_op jit(solution)/shard_map/ppermute | solution.py:47
  317.8 2.4 collective-permute-start.46
  326.6 3.3 collective-permute-done.47
  331.6 3.5 %collective-permute-done.48 = bf16[192,384]{1,0:T(8,128)(2,1)S(1)} collective-permute-done((bf16[192,384]{1,0:T(8,128)(2,1)S(1)}, bf16[192,384]{1,0:T(8,128)(2,1)S(1)}, u32[]{:S(2)}, u32[]{:S(2)}) %collective-permute-start.48) | collective-permute-done | bytes 147488 | tf_op jit(solution)/shard_map/ppermute | solution.py:47
  (385 shorter events, 112.9 us)
Async XLA Ops:
  2.4 14.3 %collective-permute-start.2 = (bf16[10,384]{1,0:T(8,128)(2,1)S(1)}, bf16[10,384]{1,0:T(8,128)(2,1)S(1)}, u32[]{:S(2)}, u32[]{:S(2)}) collective-permute-start(bf16[10,384]{1,0:T(8,128)(2,1)S(1)} %constant_dynamic-update-slice_fusion), channel_id=1, source_target_pairs={{0,8},{8,16},{16,24},{24,0},{1,9},{9,17},{17,25},{25,1},{2,10},{10... | collective-permute-start | bytes 23048 | tf_op jit(solution)/shard_map/ppermute | solution.py:51
  5.4 11.2 %collective-permute-start.1 = (bf16[10,384]{1,0:T(8,128)(2,1)S(1)}, bf16[10,384]{1,0:T(8,128)(2,1)S(1)}, u32[]{:S(2)}, u32[]{:S(2)}) collective-permute-start(bf16[10,384]{1,0:T(8,128)(2,1)S(1)} %constant_dynamic-update-slice_fusion), channel_id=1, source_target_pairs={{0,16},{8,24},{16,0},{24,8},{1,17},{9,25},{17,1},{25,9},{2,18},{10... | collective-permute-start | bytes 23048 | tf_op jit(solution)/shard_map/ppermute | solution.py:51
  8.0 8.6 %collective-permute-start = (bf16[10,384]{1,0:T(8,128)(2,1)S(1)}, bf16[10,384]{1,0:T(8,128)(2,1)S(1)}, u32[]{:S(2)}, u32[]{:S(2)}) collective-permute-start(bf16[10,384]{1,0:T(8,128)(2,1)S(1)} %constant_dynamic-update-slice_fusion), channel_id=1, source_target_pairs={{0,24},{8,0},{16,8},{24,16},{1,25},{9,1},{17,9},{25,17},{2,26},{10... | collective-permute-start | bytes 23048 | tf_op jit(solution)/shard_map/ppermute | solution.py:51
  11.7 27.0 %collective-permute-start.8 = (bf16[144,384]{1,0:T(8,128)(2,1)}, bf16[144,384]{1,0:T(8,128)(2,1)S(1)}, u32[]{:S(2)}, u32[]{:S(2)}) collective-permute-start(bf16[144,384]{1,0:T(8,128)(2,1)} %constant_dynamic-slice_fusion.6), channel_id=1, source_target_pairs={{0,8},{8,16},{16,24},{24,0},{1,9},{9,17},{17,25},{25,1},{2,10},{10... | collective-permute-start | bytes 331784 | tf_op jit(solution)/shard_map/ppermute | solution.py:51
  12.4 27.5 %collective-permute-start.7 = (bf16[144,384]{1,0:T(8,128)(2,1)}, bf16[144,384]{1,0:T(8,128)(2,1)}, u32[]{:S(2)}, u32[]{:S(2)}) collective-permute-start(bf16[144,384]{1,0:T(8,128)(2,1)} %constant_dynamic-slice_fusion.6), channel_id=1, source_target_pairs={{0,16},{8,24},{16,0},{24,8},{1,17},{9,25},{17,1},{25,9},{2,18},{10... | collective-permute-start | bytes 331784 | tf_op jit(solution)/shard_map/ppermute | solution.py:51
  17.3 7.9 %collective-permute-start.20 = (bf16[32,96]{1,0:T(8,128)(2,1)S(1)}, bf16[32,96]{1,0:T(8,128)(2,1)S(1)}, u32[]{:S(2)}, u32[]{:S(2)}) collective-permute-start(bf16[32,96]{1,0:T(8,128)(2,1)S(1)} %multiply_convert_fusion.4), channel_id=1, source_target_pairs={{0,4},{1,5},{2,6},{3,7},{4,0},{5,1},{6,2},{7,3},{8,12},{9,13},{10,... | collective-permute-start | bytes 18440 | tf_op jit(solution)/shard_map/ppermute | solution.py:47
  21.3 9.3 %collective-permute-start.3 = (f32[8,2304]{1,0:T(8,128)S(1)}, f32[8,2304]{1,0:T(8,128)S(1)}, u32[]{:S(2)}, u32[]{:S(2)}) collective-permute-start(f32[8,2304]{1,0:T(8,128)S(1)} %get-tuple-element.77), channel_id=1, source_target_pairs={{0,8},{8,16},{16,24},{24,0},{1,9},{9,17},{17,25},{25,1},{2,10},{10... | collective-permute-start | bytes 221192 | tf_op jit(solution)/shard_map/ppermute | solution.py:51
  24.7 8.8 %collective-permute-start.5 = (f32[8,2304]{1,0:T(8,128)S(1)}, f32[8,2304]{1,0:T(8,128)S(1)}, u32[]{:S(2)}, u32[]{:S(2)}) collective-permute-start(f32[8,2304]{1,0:T(8,128)S(1)} %get-tuple-element.78), channel_id=1, source_target_pairs={{0,24},{8,0},{16,8},{24,16},{1,25},{9,1},{17,9},{25,17},{2,26},{10... | collective-permute-start | bytes 221192 | tf_op jit(solution)/shard_map/ppermute | solution.py:51
  25.2 3.8 %collective-permute-start.21 = (bf16[64,96]{1,0:T(8,128)(2,1)S(1)}, bf16[64,96]{1,0:T(8,128)(2,1)S(1)}, u32[]{:S(2)}, u32[]{:S(2)}) collective-permute-start(bf16[64,96]{1,0:T(8,128)(2,1)S(1)} %pad_maximum_fusion.13), channel_id=1, source_target_pairs={{0,2},{1,3},{2,0},{3,1},{4,6},{5,7},{6,4},{7,5},{8,10},{9,11},{10,... | collective-permute-start | bytes 36872 | tf_op jit(solution)/shard_map/ppermute | solution.py:47
  29.0 8.8 %collective-permute-start.4 = (f32[8,2304]{1,0:T(8,128)S(1)}, f32[8,2304]{1,0:T(8,128)S(1)}, u32[]{:S(2)}, u32[]{:S(2)}) collective-permute-start(f32[8,2304]{1,0:T(8,128)S(1)} %get-tuple-element.79), channel_id=1, source_target_pairs={{0,16},{8,24},{16,0},{24,8},{1,17},{9,25},{17,1},{25,9},{2,18},{10... | collective-permute-start | bytes 221192 | tf_op jit(solution)/shard_map/ppermute | solution.py:51
  30.6 11.4 %collective-permute-start.6 = (bf16[144,384]{1,0:T(8,128)(2,1)}, bf16[144,384]{1,0:T(8,128)(2,1)S(1)}, u32[]{:S(2)}, u32[]{:S(2)}) collective-permute-start(bf16[144,384]{1,0:T(8,128)(2,1)} %constant_dynamic-slice_fusion.6), channel_id=1, source_target_pairs={{0,24},{8,0},{16,8},{24,16},{1,25},{9,1},{17,9},{25,17},{2,26},{10... | collective-permute-start | bytes 331784 | tf_op jit(solution)/shard_map/ppermute | solution.py:51
  33.5 17.2 %collective-permute-start.12 = (bf16[432,384]{1,0:T(8,128)(2,1)}, bf16[432,384]{1,0:T(8,128)(2,1)S(1)}, u32[]{:S(2)}, u32[]{:S(2)}) collective-permute-start(bf16[432,384]{1,0:T(8,128)(2,1)} %constant_dynamic-slice_fusion.4), channel_id=1, source_target_pairs={{0,8},{8,16},{16,24},{24,0},{1,9},{9,17},{17,25},{25,1},{2,10},{10... | collective-permute-start | bytes 995336 | tf_op jit(solution)/shard_map/ppermute | solution.py:51
  37.8 21.7 %collective-permute-start.11 = (bf16[432,384]{1,0:T(8,128)(2,1)}, bf16[432,384]{1,0:T(8,128)(2,1)S(1)}, u32[]{:S(2)}, u32[]{:S(2)}) collective-permute-start(bf16[432,384]{1,0:T(8,128)(2,1)} %constant_dynamic-slice_fusion.4), channel_id=1, source_target_pairs={{0,16},{8,24},{16,0},{24,8},{1,17},{9,25},{17,1},{25,9},{2,18},{10... | collective-permute-start | bytes 995336 | tf_op jit(solution)/shard_map/ppermute | solution.py:51
  38.7 20.8 %collective-permute-start.10 = (bf16[432,384]{1,0:T(8,128)(2,1)}, bf16[432,384]{1,0:T(8,128)(2,1)}, u32[]{:S(2)}, u32[]{:S(2)}) collective-permute-start(bf16[432,384]{1,0:T(8,128)(2,1)} %constant_dynamic-slice_fusion.4), channel_id=1, source_target_pairs={{0,24},{8,0},{16,8},{24,16},{1,25},{9,1},{17,9},{25,17},{2,26},{10... | collective-permute-start | bytes 995336 | tf_op jit(solution)/shard_map/ppermute | solution.py:51
  44.4 17.2 %collective-permute-start.9 = (bf16[3,144,384]{2,1,0:T(8,128)(2,1)}, bf16[3,144,384]{2,1,0:T(8,128)(2,1)}, u32[]{:S(2)}, u32[]{:S(2)}) collective-permute-start(bf16[3,144,384]{2,1,0:T(8,128)(2,1)} %pad_maximum_fusion.4), channel_id=1, source_target_pairs={{0,1},{1,0},{2,3},{3,2},{4,5},{5,4},{6,7},{7,6},{8,9},{9,8},{10,11... | collective-permute-start | bytes 995336 | tf_op jit(solution)/shard_map/ppermute | solution.py:47
  61.6 27.4 %collective-permute-start.13 = (bf16[3,432,384]{2,1,0:T(8,128)(2,1)}, bf16[3,432,384]{2,1,0:T(8,128)(2,1)}, u32[]{:S(2)}, u32[]{:S(2)}) collective-permute-start(bf16[3,432,384]{2,1,0:T(8,128)(2,1)} %pad_maximum_fusion.1), channel_id=1, source_target_pairs={{0,1},{1,0},{2,3},{3,2},{4,5},{5,4},{6,7},{7,6},{8,9},{9,8},{10,11... | collective-permute-start | bytes 2985992 | tf_op jit(solution)/shard_map/ppermute | solution.py:47
  208.7 36.2 %collective-permute-start.16 = (bf16[8,2304]{1,0:T(8,128)(2,1)S(1)}, bf16[8,2304]{1,0:T(8,128)(2,1)S(1)}, u32[]{:S(2)}, u32[]{:S(2)}) collective-permute-start(bf16[8,2304]{1,0:T(8,128)(2,1)S(1)} %get-tuple-element.105), channel_id=1, source_target_pairs={{0,8},{8,16},{16,24},{24,0},{1,9},{9,17},{17,25},{25,1},{2,10},{10... | collective-permute-start | bytes 110600 | tf_op jit(solution)/shard_map/ppermute | solution.py:51
  214.5 30.6 %collective-permute-start.15 = (bf16[8,2304]{1,0:T(8,128)(2,1)S(1)}, bf16[8,2304]{1,0:T(8,128)(2,1)S(1)}, u32[]{:S(2)}, u32[]{:S(2)}) collective-permute-start(bf16[8,2304]{1,0:T(8,128)(2,1)S(1)} %get-tuple-element.105), channel_id=1, source_target_pairs={{0,16},{8,24},{16,0},{24,8},{1,17},{9,25},{17,1},{25,9},{2,18},{10... | collective-permute-start | bytes 110600 | tf_op jit(solution)/shard_map/ppermute | solution.py:51
  214.8 34.2 %collective-permute-start.14 = (bf16[8,2304]{1,0:T(8,128)(2,1)S(1)}, bf16[8,2304]{1,0:T(8,128)(2,1)S(1)}, u32[]{:S(2)}, u32[]{:S(2)}) collective-permute-start(bf16[8,2304]{1,0:T(8,128)(2,1)S(1)} %get-tuple-element.105), channel_id=1, source_target_pairs={{0,24},{8,0},{16,8},{24,16},{1,25},{9,1},{17,9},{25,17},{2,26},{10... | collective-permute-start | bytes 110600 | tf_op jit(solution)/shard_map/ppermute | solution.py:51
  231.4 55.1 %collective-permute-start.41 = (bf16[4,384,384]{2,1,0:T(8,128)(2,1)}, bf16[4,384,384]{2,1,0:T(8,128)(2,1)}, u32[]{:S(2)}, u32[]{:S(2)}) collective-permute-start(bf16[4,384,384]{2,1,0:T(8,128)(2,1)} %dynamic-slice_convert_fusion), channel_id=1, source_target_pairs={{0,1},{1,0},{2,3},{3,2},{4,5},{5,4},{6,7},{7,6},{8,9},{9,8},{10,11... | collective-permute-start | bytes 3538952 | tf_op jit(solution)/shard_map/ppermute | solution.py:47
  231.7 5.7 %collective-permute-start.35 = (f32[4,768]{1,0:T(4,128)S(1)}, f32[4,768]{1,0:T(4,128)S(1)}, u32[]{:S(2)}, u32[]{:S(2)}) collective-permute-start(f32[4,768]{1,0:T(4,128)S(1)} %pad_maximum_fusion.14), channel_id=1, source_target_pairs={{0,1},{1,0},{2,3},{3,2},{4,5},{5,4},{6,7},{7,6},{8,9},{9,8},{10,11... | collective-permute-start | bytes 36872 | tf_op jit(solution)/shard_map/ppermute | solution.py:47
  237.5 3.7 %collective-permute-start.36 = (f32[4,768]{1,0:T(4,128)S(1)}, f32[4,768]{1,0:T(4,128)S(1)}, u32[]{:S(2)}, u32[]{:S(2)}) collective-permute-start(f32[4,768]{1,0:T(4,128)S(1)} %fusion.136), channel_id=1, source_target_pairs={{0,2},{1,3},{2,0},{3,1},{4,6},{5,7},{6,4},{7,5},{8,10},{9,11},{10,... | collective-permute-start | bytes 36872 | tf_op jit(solution)/shard_map/ppermute | solution.py:47
  244.9 15.6 %collective-permute-start.26 = (bf16[4,192,384]{2,1,0:T(8,128)(2,1)}, bf16[4,192,384]{2,1,0:T(8,128)(2,1)}, u32[]{:S(2)}, u32[]{:S(2)}) collective-permute-start(bf16[4,192,384]{2,1,0:T(8,128)(2,1)} %dynamic-slice_convert_fusion.2), channel_id=1, source_target_pairs={{0,1},{1,0},{2,3},{3,2},{4,5},{5,4},{6,7},{7,6},{8,9},{9,8},{10,11... | collective-permute-start | bytes 1769480 | tf_op jit(solution)/shard_map/ppermute | solution.py:47
  245.0 7.2 %collective-permute-start.38 = (f32[768]{0:T(1024)S(1)}, f32[768]{0:T(1024)S(1)}, u32[]{:S(2)}, u32[]{:S(2)}) collective-permute-start(f32[768]{0:T(1024)S(1)} %get-tuple-element.19), channel_id=1, source_target_pairs={{0,8},{8,16},{16,24},{24,0},{1,9},{9,17},{17,25},{25,1},{2,10},{10... | collective-permute-start | bytes 9224 | tf_op jit(solution)/shard_map/ppermute | solution.py:51
  245.0 8.0 %collective-permute-start.40 = (f32[768]{0:T(1024)S(1)}, f32[768]{0:T(1024)S(1)}, u32[]{:S(2)}, u32[]{:S(2)}) collective-permute-start(f32[768]{0:T(1024)S(1)} %get-tuple-element.20), channel_id=1, source_target_pairs={{0,24},{8,0},{16,8},{24,16},{1,25},{9,1},{17,9},{25,17},{2,26},{10... | collective-permute-start | bytes 9224 | tf_op jit(solution)/shard_map/ppermute | solution.py:51
  249.0 6.2 %collective-permute-start.39 = (f32[768]{0:T(1024)S(1)}, f32[768]{0:T(1024)S(1)}, u32[]{:S(2)}, u32[]{:S(2)}) collective-permute-start(f32[768]{0:T(1024)S(1)} %get-tuple-element.21), channel_id=1, source_target_pairs={{0,16},{8,24},{16,0},{24,8},{1,17},{9,25},{17,1},{25,9},{2,18},{10... | collective-permute-start | bytes 9224 | tf_op jit(solution)/shard_map/ppermute | solution.py:51
  252.2 8.2 %collective-permute-start.19 = (f32[8,96]{1,0:T(8,128)S(1)}, f32[8,96]{1,0:T(8,128)S(1)}, u32[]{:S(2)}, u32[]{:S(2)}) collective-permute-start(f32[8,96]{1,0:T(8,128)S(1)} %get-tuple-element.97), channel_id=1, source_target_pairs={{0,8},{8,16},{16,24},{24,0},{1,9},{9,17},{17,25},{25,1},{2,10},{10... | collective-permute-start | bytes 9224 | tf_op jit(solution)/shard_map/ppermute | solution.py:51
  253.0 7.4 %collective-permute-start.18 = (f32[8,96]{1,0:T(8,128)S(1)}, f32[8,96]{1,0:T(8,128)S(1)}, u32[]{:S(2)}, u32[]{:S(2)}) collective-permute-start(f32[8,96]{1,0:T(8,128)S(1)} %get-tuple-element.98), channel_id=1, source_target_pairs={{0,16},{8,24},{16,0},{24,8},{1,17},{9,25},{17,1},{25,9},{2,18},{10... | collective-permute-start | bytes 9224 | tf_op jit(solution)/shard_map/ppermute | solution.py:51
  255.2 4.6 %collective-permute-start.17 = (f32[8,96]{1,0:T(8,128)S(1)}, f32[8,96]{1,0:T(8,128)S(1)}, u32[]{:S(2)}, u32[]{:S(2)}) collective-permute-start(f32[8,96]{1,0:T(8,128)S(1)} %get-tuple-element.99), channel_id=1, source_target_pairs={{0,24},{8,0},{16,8},{24,16},{1,25},{9,1},{17,9},{25,17},{2,26},{10... | collective-permute-start | bytes 9224 | tf_op jit(solution)/shard_map/ppermute | solution.py:51
  259.9 5.1 %collective-permute-start.23 = (bf16[32,2304]{1,0:T(8,128)(2,1)S(1)}, bf16[32,2304]{1,0:T(8,128)(2,1)S(1)}, u32[]{:S(2)}, u32[]{:S(2)}) collective-permute-start(bf16[32,2304]{1,0:T(8,128)(2,1)S(1)} %pad_maximum_fusion.8), channel_id=1, source_target_pairs={{0,4},{1,5},{2,6},{3,7},{4,0},{5,1},{6,2},{7,3},{8,12},{9,13},{10,... | collective-permute-start | bytes 442376 | tf_op jit(solution)/shard_map/ppermute | solution.py:47
  262.1 10.0 %collective-permute-start.27 = (bf16[4,96,384]{2,1,0:T(8,128)(2,1)S(1)}, bf16[4,96,384]{2,1,0:T(8,128)(2,1)S(1)}, u32[]{:S(2)}, u32[]{:S(2)}) collective-permute-start(bf16[4,96,384]{2,1,0:T(8,128)(2,1)S(1)} %dynamic-slice_convert_fusion.4), channel_id=1, source_target_pairs={{0,2},{1,3},{2,0},{3,1},{4,6},{5,7},{6,4},{7,5},{8,10},{9,11},{10,... | collective-permute-start | bytes 884744 | tf_op jit(solution)/shard_map/ppermute | solution.py:47
  265.7 10.6 %collective-permute-start.24 = (bf16[64,2304]{1,0:T(8,128)(2,1)}, bf16[64,2304]{1,0:T(8,128)(2,1)S(1)}, u32[]{:S(2)}, u32[]{:S(2)}) collective-permute-start(bf16[64,2304]{1,0:T(8,128)(2,1)} %constant_dynamic-update-slice_fusion.30), channel_id=1, source_target_pairs={{0,2},{1,3},{2,0},{3,1},{4,6},{5,7},{6,4},{7,5},{8,10},{9,11},{10,... | collective-permute-start | bytes 884744 | tf_op jit(solution)/shard_map/ppermute | solution.py:47
  273.7 7.8 %collective-permute-start.28 = (bf16[4,48,384]{2,1,0:T(8,128)(2,1)}, bf16[4,48,384]{2,1,0:T(8,128)(2,1)S(1)}, u32[]{:S(2)}, u32[]{:S(2)}) collective-permute-start(bf16[4,48,384]{2,1,0:T(8,128)(2,1)} %dynamic-slice_convert_fusion.5), channel_id=1, source_target_pairs={{0,4},{1,5},{2,6},{3,7},{4,0},{5,1},{6,2},{7,3},{8,12},{9,13},{10,... | collective-permute-start | bytes 442376 | tf_op jit(solution)/shard_map/ppermute | solution.py:47
  281.5 12.8 %collective-permute-start.25 = (bf16[128,2304]{0,1:T(8,128)(2,1)}, bf16[128,2304]{0,1:T(8,128)(2,1)}, u32[]{:S(2)}, u32[]{:S(2)}) collective-permute-start(bf16[128,2304]{0,1:T(8,128)(2,1)} %concatenate.123), channel_id=1, source_target_pairs={{0,1},{1,0},{2,3},{3,2},{4,5},{5,4},{6,7},{7,6},{8,9},{9,8},{10,11... | collective-permute-start | bytes 1769480 | tf_op jit(solution)/shard_map/ppermute | solution.py:47
  282.5 10.7 %collective-permute-start.29 = (bf16[48,384]{1,0:T(8,128)(2,1)S(1)}, bf16[48,384]{1,0:T(8,128)(2,1)S(1)}, u32[]{:S(2)}, u32[]{:S(2)}) collective-permute-start(bf16[48,384]{1,0:T(8,128)(2,1)S(1)} %get-tuple-element.74), channel_id=1, source_target_pairs={{0,8},{8,16},{16,24},{24,0},{1,9},{9,17},{17,25},{25,1},{2,10},{10... | collective-permute-start | bytes 110600 | tf_op jit(solution)/shard_map/ppermute | solution.py:51
  282.9 10.2 %collective-permute-start.31 = (bf16[48,384]{1,0:T(8,128)(2,1)S(1)}, bf16[48,384]{1,0:T(8,128)(2,1)S(1)}, u32[]{:S(2)}, u32[]{:S(2)}) collective-permute-start(bf16[48,384]{1,0:T(8,128)(2,1)S(1)} %get-tuple-element.75), channel_id=1, source_target_pairs={{0,24},{8,0},{16,8},{24,16},{1,25},{9,1},{17,9},{25,17},{2,26},{10... | collective-permute-start | bytes 110600 | tf_op jit(solution)/shard_map/ppermute | solution.py:51
  286.4 6.8 %collective-permute-start.30 = (bf16[48,384]{1,0:T(8,128)(2,1)S(1)}, bf16[48,384]{1,0:T(8,128)(2,1)S(1)}, u32[]{:S(2)}, u32[]{:S(2)}) collective-permute-start(bf16[48,384]{1,0:T(8,128)(2,1)S(1)} %get-tuple-element.76), channel_id=1, source_target_pairs={{0,16},{8,24},{16,0},{24,8},{1,17},{9,25},{17,1},{25,9},{2,18},{10... | collective-permute-start | bytes 110600 | tf_op jit(solution)/shard_map/ppermute | solution.py:51
  291.1 15.5 %collective-permute-start.42 = (bf16[4,192,384]{2,1,0:T(8,128)(2,1)}, bf16[4,192,384]{2,1,0:T(8,128)(2,1)}, u32[]{:S(2)}, u32[]{:S(2)}) collective-permute-start(bf16[4,192,384]{2,1,0:T(8,128)(2,1)} %dynamic-slice_convert_fusion.1), channel_id=1, source_target_pairs={{0,2},{1,3},{2,0},{3,1},{4,6},{5,7},{6,4},{7,5},{8,10},{9,11},{10,... | collective-permute-start | bytes 1769480 | tf_op jit(solution)/shard_map/ppermute | solution.py:47
  293.2 6.1 %collective-permute-start.22 = (bf16[128,96]{1,0:T(8,128)(2,1)S(1)}, bf16[128,96]{1,0:T(8,128)(2,1)S(1)}, u32[]{:S(2)}, u32[]{:S(2)}) collective-permute-start(bf16[128,96]{1,0:T(8,128)(2,1)S(1)} %copy-done.55), channel_id=1, source_target_pairs={{0,1},{1,0},{2,3},{3,2},{4,5},{5,4},{6,7},{7,6},{8,9},{9,8},{10,11... | collective-permute-start | bytes 73736 | tf_op jit(solution)/shard_map/ppermute | solution.py:47
  293.2 16.0 %collective-permute-start.32 = (bf16[48,384]{1,0:T(8,128)(2,1)S(1)}, bf16[48,384]{1,0:T(8,128)(2,1)S(1)}, u32[]{:S(2)}, u32[]{:S(2)}) collective-permute-start(bf16[48,384]{1,0:T(8,128)(2,1)S(1)} %fusion.63), channel_id=1, source_target_pairs={{0,4},{1,5},{2,6},{3,7},{4,0},{5,1},{6,2},{7,3},{8,12},{9,13},{10,... | collective-permute-start | bytes 110600 | tf_op jit(solution)/shard_map/ppermute | solution.py:47
  308.2 8.1 %collective-permute-start.43 = (bf16[4,96,384]{2,1,0:T(8,128)(2,1)S(1)}, bf16[4,96,384]{2,1,0:T(8,128)(2,1)S(1)}, u32[]{:S(2)}, u32[]{:S(2)}) collective-permute-start(bf16[4,96,384]{2,1,0:T(8,128)(2,1)S(1)} %dynamic-slice_convert_fusion.3), channel_id=1, source_target_pairs={{0,4},{1,5},{2,6},{3,7},{4,0},{5,1},{6,2},{7,3},{8,12},{9,13},{10,... | collective-permute-start | bytes 884744 | tf_op jit(solution)/shard_map/ppermute | solution.py:47
  309.2 11.3 %collective-permute-start.33 = (bf16[96,384]{1,0:T(8,128)(2,1)S(1)}, bf16[96,384]{1,0:T(8,128)(2,1)S(1)}, u32[]{:S(2)}, u32[]{:S(2)}) collective-permute-start(bf16[96,384]{1,0:T(8,128)(2,1)S(1)} %pad_maximum_fusion.11), channel_id=1, source_target_pairs={{0,2},{1,3},{2,0},{3,1},{4,6},{5,7},{6,4},{7,5},{8,10},{9,11},{10,... | collective-permute-start | bytes 221192 | tf_op jit(solution)/shard_map/ppermute | solution.py:47
  316.3 6.4 %collective-permute-start.44 = (bf16[96,384]{1,0:T(8,128)(2,1)S(1)}, bf16[96,384]{1,0:T(8,128)(2,1)S(1)}, u32[]{:S(2)}, u32[]{:S(2)}) collective-permute-start(bf16[96,384]{1,0:T(8,128)(2,1)S(1)} %get-tuple-element.63), channel_id=1, source_target_pairs={{0,8},{8,16},{16,24},{24,0},{1,9},{9,17},{17,25},{25,1},{2,10},{10... | collective-permute-start | bytes 221192 | tf_op jit(solution)/shard_map/ppermute | solution.py:51
  317.8 5.9 %collective-permute-start.46 = (bf16[96,384]{1,0:T(8,128)(2,1)S(1)}, bf16[96,384]{1,0:T(8,128)(2,1)S(1)}, u32[]{:S(2)}, u32[]{:S(2)}) collective-permute-start(bf16[96,384]{1,0:T(8,128)(2,1)S(1)} %get-tuple-element.64), channel_id=1, source_target_pairs={{0,24},{8,0},{16,8},{24,16},{1,25},{9,1},{17,9},{25,17},{2,26},{10... | collective-permute-start | bytes 221192 | tf_op jit(solution)/shard_map/ppermute | solution.py:51
  320.2 5.3 %collective-permute-start.45 = (bf16[96,384]{1,0:T(8,128)(2,1)S(1)}, bf16[96,384]{1,0:T(8,128)(2,1)S(1)}, u32[]{:S(2)}, u32[]{:S(2)}) collective-permute-start(bf16[96,384]{1,0:T(8,128)(2,1)S(1)} %get-tuple-element.65), channel_id=1, source_target_pairs={{0,16},{8,24},{16,0},{24,8},{1,17},{9,25},{17,1},{25,9},{2,18},{10... | collective-permute-start | bytes 221192 | tf_op jit(solution)/shard_map/ppermute | solution.py:51
  325.5 4.4 %collective-permute-start.47 = (bf16[96,384]{1,0:T(8,128)(2,1)S(1)}, bf16[96,384]{1,0:T(8,128)(2,1)S(1)}, u32[]{:S(2)}, u32[]{:S(2)}) collective-permute-start(bf16[96,384]{1,0:T(8,128)(2,1)S(1)} %fusion.55), channel_id=1, source_target_pairs={{0,4},{1,5},{2,6},{3,7},{4,0},{5,1},{6,2},{7,3},{8,12},{9,13},{10,... | collective-permute-start | bytes 221192 | tf_op jit(solution)/shard_map/ppermute | solution.py:47
  326.6 5.0 %collective-permute-start.34 = (bf16[192,384]{1,0:T(8,128)(2,1)S(1)}, bf16[192,384]{1,0:T(8,128)(2,1)S(1)}, u32[]{:S(2)}, u32[]{:S(2)}) collective-permute-start(bf16[192,384]{1,0:T(8,128)(2,1)S(1)} %pad_maximum_fusion.9), channel_id=1, source_target_pairs={{0,1},{1,0},{2,3},{3,2},{4,5},{5,4},{6,7},{7,6},{8,9},{9,8},{10,11... | collective-permute-start | bytes 442376 | tf_op jit(solution)/shard_map/ppermute | solution.py:47
  330.0 5.2 %collective-permute-start.48 = (bf16[192,384]{1,0:T(8,128)(2,1)S(1)}, bf16[192,384]{1,0:T(8,128)(2,1)S(1)}, u32[]{:S(2)}, u32[]{:S(2)}) collective-permute-start(bf16[192,384]{1,0:T(8,128)(2,1)S(1)} %pad_maximum_fusion.10), channel_id=1, source_target_pairs={{0,2},{1,3},{2,0},{3,1},{4,6},{5,7},{6,4},{7,5},{8,10},{9,11},{10,... | collective-permute-start | bytes 442376 | tf_op jit(solution)/shard_map/ppermute | solution.py:47
  (72 other events, 604.8 us)

commit v2 on v1

--- a/solution.py
+++ b/solution.py
@@ -1,6 +1,10 @@
+import functools
+
 import jax
 import jax.numpy as jnp
 from jax import lax
+from jax.experimental import pallas as pl
+from jax.experimental.pallas import tpu as pltpu
 from jax.sharding import PartitionSpec as P
 
 HEAD_DIM = 64
@@ -101,40 +105,217 @@
     return in_order([rows] + [joined[i] for i in range(shard_count - 1)], shard_at)
 
 
-def reduce_rows(partial, shard_count, shard_at, rep_count, rep_at):
-    kept = partial
-    bits = rep_bits(rep_count)
-    for at, bit in enumerate(bits):
-        side = (rep_at >> at) & 1
-        half = kept.shape[1] // 2
-        sent = lax.dynamic_slice_in_dim(kept, (1 - side) * half, half, axis=1)
-        came = swap_rep(sent.astype(jnp.bfloat16), bit, rep_count)
-        kept = lax.dynamic_slice_in_dim(kept, side * half, half, axis=1) + came.astype(jnp.float32)
-    total = lax.dynamic_index_in_dim(kept, shard_at, 0, keepdims=False)
-    for hop in range(1, shard_count):
-        target = (shard_at + hop) % shard_count
-        sent = lax.dynamic_index_in_dim(kept, target, 0, keepdims=False)
-        came = to_shard(sent.astype(jnp.bfloat16), hop, shard_count)
-        total = total + came.astype(jnp.float32)
-    whole = total.astype(jnp.bfloat16)
-    for at in range(len(bits) - 1, -1, -1):
-        side = (rep_at >> at) & 1
-        other = swap_rep(whole, bits[at], rep_count)
-        whole = jnp.concatenate(
-            [jnp.where(side == 0, whole, other), jnp.where(side == 0, other, whole)], axis=0
+def reduce_kernel(
+    shard_count, rep_count, plans, half_mod, lane_total, *refs
+):
+    refs = list(refs)
+    lane_refs = [refs.pop(0) for _ in range(lane_total)]
+    small_ref, mod_ref, ada_ref = refs.pop(0), refs.pop(0), refs.pop(0)
+    lane_outs = [refs.pop(0) for _ in range(lane_total)]
+    small_out, mod_out, cond_out = refs.pop(0), refs.pop(0), refs.pop(0)
+    bits_total = rep_count.bit_length() - 1
+    lane_bufs = []
+    for _ in range(lane_total):
+        stages = [[refs.pop(0) for _ in range(3)] for _ in range(bits_total)]
+        lane_bufs.append((stages, refs.pop(0), refs.pop(0), refs.pop(0)))
+    small_acc, small_came, small_z = refs.pop(0), refs.pop(0), refs.pop(0)
+    mod_buf, cond_send, cond_came = refs.pop(0), refs.pop(0), refs.pop(0)
+    send_sems, recv_sems = refs
+    shard_at, rep_at = lax.axis_index("shard"), lax.axis_index("rep")
+    bits = [1 << i for i in range(bits_total)]
+    sides = [lax.rem(rep_at // bit, 2) for bit in bits]
+    peers = [rep_at + bit - 2 * bit * side for bit, side in zip(bits, sides)]
+    targets = [lax.rem(shard_at + hop, shard_count) for hop in range(shard_count)]
+
+    barrier = pltpu.get_barrier_semaphore()
+    partners = [{"rep": peer} for peer in peers] + [{"shard": at} for at in targets[1:]]
+    for partner in partners:
+        pl.semaphore_signal(
+            barrier, inc=1, device_id=partner, device_id_type=pl.DeviceIdType.MESH
         )
-    return whole.astype(jnp.float32)
-
-
-def sum_small(partial, shard_count, shard_at, rep_count):
-    for bit in rep_bits(rep_count):
-        partial = partial + swap_rep(partial, bit, rep_count)
-    total = lax.dynamic_index_in_dim(partial, shard_at, 0, keepdims=False)
-    for hop in range(1, shard_count):
-        target = (shard_at + hop) % shard_count
-        sent = lax.dynamic_index_in_dim(partial, target, 0, keepdims=False)
-        total = total + to_shard(sent, hop, shard_count)
-    return total
+    pl.semaphore_wait(barrier, len(partners))
+    used = [0]
+
+    def send(source, landing, partner):
+        at = used[0]
+        used[0] += 1
+        copy = pltpu.make_async_remote_copy(
+            src_ref=source,
+            dst_ref=landing,
+            send_sem=send_sems.at[at],
+            recv_sem=recv_sems.at[at],
+            device_id=partner,
+            device_id_type=pl.DeviceIdType.MESH,
+        )
+        copy.start()
+        return copy
+
+    def lane_steps(lane):
+        (order, halved), source = plans[lane], lane_refs[lane]
+        stages, z_send, z_came, final = lane_bufs[lane]
+        offset = 0
+        for at, split, (sent, came, kept) in zip(order, halved, stages):
+            rows = sent.shape[1]
+            side = sides[at]
+            if split:
+                away = pl.multiple_of((1 - side) * rows, 16)
+                stay = pl.multiple_of(side * rows, 16)
+                sent[...] = source[:, pl.ds(away, rows), :].astype(jnp.bfloat16)
+            else:
+                sent[...] = source[...].astype(jnp.bfloat16)
+            copy = send(sent, came, {"rep": peers[at]})
+            yield
+            copy.wait()
+            if split:
+                kept[...] = source[:, pl.ds(stay, rows), :] + came[...].astype(jnp.float32)
+                offset = offset + side * rows
+            else:
+                kept[...] = sent[...].astype(jnp.float32) + came[...].astype(jnp.float32)
+            source = kept
+        z_send[...] = source[...].astype(jnp.bfloat16)
+        copies = [
+            send(z_send.at[targets[hop]], z_came.at[hop - 1], {"shard": targets[hop]})
+            for hop in range(1, shard_count)
+        ]
+        yield
+        total = source[shard_at]
+        for copy in copies:
+            copy.wait()
+        for hop in range(1, shard_count):
+            total = total + z_came[hop - 1].astype(jnp.float32)
+        rows = total.shape[0]
+        final[pl.ds(pl.multiple_of(offset, 16), rows), :] = total.astype(jnp.bfloat16)
+        for at, split in list(zip(order, halved))[::-1]:
+            if not split:
+                continue
+            place = final.at[pl.ds(pl.multiple_of(offset, 16), rows), :]
+            copy = send(place, place, {"rep": peers[at]})
+            yield
+            copy.wait()
+            offset = offset - sides[at] * rows
+            rows = rows * 2
+        lane_outs[lane][...] = final[...].astype(jnp.float32)
+
+    def small_steps():
+        small_acc[0] = small_ref[...]
+        for at in range(bits_total):
+            copy = send(small_acc.at[at], small_came.at[at], {"rep": peers[at]})
+            yield
+            copy.wait()
+            small_acc[at + 1] = small_acc[at] + small_came[at]
+        copies = [
+            send(
+                small_acc.at[bits_total, targets[hop]],
+                small_z.at[hop - 1],
+                {"shard": targets[hop]},
+            )
+            for hop in range(1, shard_count)
+        ]
+        yield
+        total = small_acc[bits_total, shard_at]
+        for copy in copies:
+            copy.wait()
+        for hop in range(1, shard_count):
+            total = total + small_z[hop - 1]
+        small_out[...] = total
+
+    def mod_steps():
+        mod_buf[0] = mod_ref[...]
+        copies = [
+            send(mod_buf.at[0], mod_buf.at[shard_count - hop], {"shard": targets[hop]})
+            for hop in range(1, shard_count)
+        ]
+        yield
+        for copy in copies:
+            copy.wait()
+        filled = shard_count
+        copy = None
+        cond_copies = []
+        for at in range(bits_total)[::-1]:
+            copy = send(
+                mod_buf.at[pl.ds(0, filled)], mod_buf.at[pl.ds(filled, filled)], {"rep": peers[at]}
+            )
+            if filled == shard_count:
+                for near in range(shard_count):
+                    rows = mod_buf[near][:, :half_mod]
+                    dims = (((1,), (1,)), ((), ()))
+                    first = lax.dot_general(
+                        rows, ada_ref[:, :half_mod], dims, preferred_element_type=jnp.float32
+                    )
+                    second = lax.dot_general(
+                        rows, ada_ref[:, half_mod:], dims, preferred_element_type=jnp.float32
+                    )
+                    lat = rows.shape[0] // 2
+                    cond_send[near] = first[:lat] + second[lat:]
+                cond_copies = [
+                    send(cond_send.at[hop], cond_came.at[hop - 1], {"shard": targets[hop]})
+                    for hop in range(1, shard_count)
+                ]
+            yield
+            copy.wait()
+            filled = filled * 2
+        for done in cond_copies:
+            done.wait()
+        cond_out[0] = cond_send[0]
+        for hop in range(1, shard_count):
+            cond_out[hop] = cond_came[hop - 1]
+        mod_out[...] = mod_buf[...]
+
+    running = [lane_steps(lane) for lane in range(lane_total)] + [mod_steps(), small_steps()]
+    while running:
+        running = [steps for steps in running if next(steps, "end") is None]
+
+
+def reduce_all(lanes, small, mod_slot, ada_padded, shard_count, rep_count, half_mod):
+    bits_total = rep_count.bit_length() - 1
+    plans, scratch, outs = [], [], []
+    copies = 0
+    for at, lane in enumerate(lanes):
+        count, rows, width = lane.shape
+        order = list(range(bits_total))
+        if at % 2 == 1:
+            order = order[:1] + order[:0:-1]
+        halved = []
+        for _ in order:
+            split = rows % 32 == 0
+            halved.append(split)
+            rows = rows // 2 if split else rows
+            scratch.append(pltpu.VMEM((count, rows, width), jnp.bfloat16))
+            scratch.append(pltpu.VMEM((count, rows, width), jnp.bfloat16))
+            scratch.append(pltpu.VMEM((count, rows, width), jnp.float32))
+        scratch.append(pltpu.VMEM((count, rows, width), jnp.bfloat16))
+        scratch.append(pltpu.VMEM((count - 1, rows, width), jnp.bfloat16))
+        scratch.append(pltpu.VMEM((lane.shape[1], width), jnp.bfloat16))
+        plans.append((order, halved))
+        outs.append(jax.ShapeDtypeStruct((lane.shape[1], width), jnp.float32))
+        copies += 2 * bits_total + shard_count
+    slots = shard_count * rep_count
+    lat = mod_slot.shape[0] // 2
+    scratch += [
+        pltpu.VMEM((bits_total + 1,) + small.shape, jnp.float32),
+        pltpu.VMEM((bits_total,) + small.shape, jnp.float32),
+        pltpu.VMEM((shard_count - 1,) + small.shape[1:], jnp.float32),
+        pltpu.VMEM((slots,) + mod_slot.shape, jnp.bfloat16),
+        pltpu.VMEM((shard_count, lat, 128), jnp.float32),
+        pltpu.VMEM((shard_count - 1, lat, 128), jnp.float32),
+    ]
+    copies += 2 * bits_total + 3 * shard_count
+    scratch += [pltpu.SemaphoreType.DMA((copies,)), pltpu.SemaphoreType.DMA((copies,))]
+    outs += [
+        jax.ShapeDtypeStruct(small.shape[1:], jnp.float32),
+        jax.ShapeDtypeStruct((slots,) + mod_slot.shape, jnp.bfloat16),
+        jax.ShapeDtypeStruct((shard_count, lat, 128), jnp.float32),
+    ]
+    return pl.pallas_call(
+        functools.partial(reduce_kernel, shard_count, rep_count, plans, half_mod, len(lanes)),
+        out_shape=outs,
+        in_specs=[pl.BlockSpec(memory_space=pltpu.VMEM)] * (len(lanes) + 3),
+        out_specs=[pl.BlockSpec(memory_space=pltpu.VMEM)] * len(outs),
+        scratch_shapes=scratch,
+        compiler_params=pltpu.CompilerParams(
+            collective_id=0, has_side_effects=True, vmem_limit_bytes=56 * 1024 * 1024
+        ),
+    )(*lanes, small, mod_slot, ada_padded)
 
 
 def shards(
@@ -239,14 +420,6 @@
     hidden_grad = gelu_pull(project_back(down_grad, down_matrix))[0].astype(jnp.bfloat16)
     up_w_grad = weight_grad(second_low, hidden_grad)
     up_b_grad = column_sums(hidden_grad)
-    early = jnp.concatenate(
-        [
-            down_w_grad.reshape(shard_count, -1, model_width),
-            block_grad(up_w_grad, shard_count),
-        ],
-        axis=1,
-    )
-    early_sum = reduce_rows(early, shard_count, shard_at, rep_count, rep_at)
     middle_part, shift_two_grad, scale_two_grad = second_pull(project_back(hidden_grad, up_matrix))
     middle_grad = upstream + middle_part
     attn_grad = (gate_one[:, None, :] * middle_grad).astype(jnp.bfloat16)
@@ -303,7 +476,11 @@
         [proj_w_grad.reshape(shard_count, -1, model_width), block_grad(qkv_w_grad, shard_count)],
         axis=1,
     )
-    late_sum = reduce_rows(late, shard_count, shard_at, rep_count, rep_at)
+    lanes = (
+        down_w_grad.reshape(shard_count, -1, model_width),
+        block_grad(up_w_grad, shard_count),
+        late,
+    )
     small_grads = jnp.concatenate(
         [
             vector.reshape(shard_count, -1)
@@ -311,21 +488,43 @@
         ],
         axis=1,
     )
-    small_final = sum_small(small_grads, shard_count, shard_at, rep_count)
-    mod_near = jnp.concatenate(gather_near(mod_grad, shard_count), axis=0)
-    cond_part = jnp.einsum("le,de->ld", mod_near, ada_weight, preferred_element_type=jnp.float32)
-    cond_part = cond_part.reshape(shard_count, latent_count, part)
-    pieces = [cond_part[0]]
-    for hop in range(1, shard_count):
-        pieces.append(to_shard(cond_part[hop], hop, shard_count))
-    pieces = pieces[:1] + pieces[:0:-1]
-    cond_grad = in_order(pieces, shard_at)
+    small_width = small_grads.shape[1]
+    small_grads = jnp.pad(small_grads, ((0, 0), (0, 1024 - small_width)))
+    half_mod, half_silu = mod_grad.shape[1] // 2, model_width // 2
+    silu_mid = jax.nn.silu(conditioning.astype(jnp.float32)).astype(jnp.bfloat16)
+    silu_fold = jnp.concatenate([silu_mid[:, :half_silu], silu_mid[:, half_silu:]], axis=0)
+    mod_slot = jnp.concatenate(
+        [
+            jnp.concatenate([mod_grad[:, :half_mod], mod_grad[:, half_mod:]], axis=0),
+            jnp.pad(silu_fold, ((0, 0), (0, 256 - half_silu))),
+        ],
+        axis=1,
+    )
+    down_sum, up_sum, late_sum, small_final, mod_slots, cond_near_grad = reduce_all(
+        lanes,
+        small_grads.reshape(shard_count, 8, 128),
+        mod_slot,
+        jnp.pad(ada_weight, ((0, 128 - part), (0, 0))),
+        shard_count,
+        rep_count,
+        half_mod,
+    )
+    small_final = small_final.reshape(-1)
+    pieces = [cond_near_grad[i, :, :part] for i in range(shard_count)]
+    cond_grad = in_order(pieces[:1] + pieces[:0:-1], shard_at)
     cond_grad = cond_grad.transpose(1, 0, 2).reshape(latent_count, model_width)
     cond_grad = silu_pull(cond_grad)[0]
-    mod_all, silu_all = mod_near, silu_mine
-    for bit in rep_bits(rep_count)[::-1]:
-        mod_all = jnp.concatenate([mod_all, swap_rep(mod_all, bit, rep_count)], axis=0)
-        silu_all = jnp.concatenate([silu_all, swap_rep(silu_all, bit, rep_count)], axis=0)
+    top, bottom = mod_slots[:, :latent_count], mod_slots[:, latent_count:]
+    mod_all = jnp.concatenate([top[:, :, :half_mod], bottom[:, :, :half_mod]], axis=2)
+    mod_all = mod_all.reshape(-1, 2 * half_mod)
+    silu_all = jnp.concatenate(
+        [
+            top[:, :, half_mod : half_mod + half_silu],
+            bottom[:, :, half_mod : half_mod + half_silu],
+        ],
+        axis=2,
+    ).reshape(-1, model_width)
+    silu_all = lax.dynamic_slice_in_dim(silu_all, shard_at * part, part, axis=1)
     final_ada_w = jnp.einsum("ld,le->de", silu_all, mod_all, preferred_element_type=jnp.float32)
     bias_cols = ada_bias.shape[0]
     final_ada_b = jnp.sum(
@@ -333,9 +532,8 @@
         axis=0,
         dtype=jnp.float32,
     )
-    down_rows = fc2_weight.shape[0]
-    final_down_w = early_sum[:down_rows]
-    final_up_w = unblock(early_sum[down_rows:], part)
+    final_down_w = down_sum
+    final_up_w = unblock(up_sum, part)
     final_proj_w = late_sum[:part]
     final_qkv_w = unblock(late_sum[part:], part)
     final_qv_b, final_proj_b, final_up_b, final_down_b = (

time: 344 us -> 292 us (0.85)
  Pallas kernels: 0 us -> 50.9 us
  starting transfers between devices: 61.9 us -> 15.6 us
  waiting for transfers between devices: 50.1 us -> 19.9 us
  local copies, waits for them, and re-layouts: 56.8 us -> 44.2 us
  matrix products: 105 us -> 97.8 us
  other arithmetic: 62.7 us -> 57.1 us
    pallas_call x0 -> x1, Pallas kernels: none -> 50.9 us  [reduce_all(): pl.pallas_call(functools.partial(reduce_kernel, shard_count, rep_count, p...]
    ppermute x23 -> x2, waiting for transfers between devices: 30.1 us -> 0.01 us  [swap_rep(): return lax.ppermute(values, 'rep', [(i, i ^ bit) for i in range(rep_count)])]
    ppermute x27 -> x12, starting transfers between devices: 43.3 us -> 15.6 us  [to_shard(): lax.ppermute(values, 'shard', [(i, (i + hop) % shard_count) for i in rang...]
    ppermute x23 -> x2, starting transfers between devices: 18.6 us -> 0.01 us  [swap_rep(): return lax.ppermute(values, 'rep', [(i, i ^ bit) for i in range(rep_count)])]
    concatenate x5 -> x0, local copies, waits for them, and re-layouts: 9.32 us -> none  [the longest x3 8.97 us: shards(): jnp.concatenate([mod_all, swap_rep(mod_all, bit, rep_count)], axis=0)]
    unnamed x174 -> x180, local copies, waits for them, and re-layouts: 17.6 us -> 12.9 us
    dot_general x4, matrix products: 17.3 us -> 13.1 us  [weight_grad(): jnp.einsum('lsd,lse->de', inputs, gradient, preferred_element_type=jnp.fl...]
    add x10 -> x1, other arithmetic: 6.57 us -> 2.45 us  [shards(): input_grad = middle_grad + input_part]
  transfers between devices with their start and end apart: 50 -> 14, of which waited for: 16 -> 5; matrix products, arithmetic and copies ran while one was open for 27% -> 16% of each run, Pallas kernels for 0% -> 0%
where the time goes in v2:
time: 292 us; the launch traced here: 288 us
  matrix products  97.8 us (33%)
  other arithmetic  57.1 us (20%)
  Pallas kernels  50.9 us (17%)
  local copies, waits for them, and re-layouts  44.2 us (15%)
  waiting for transfers between devices  19.9 us (7%)
  starting transfers between devices  15.6 us (5%)
    pallas_call x1, Pallas kernels, reduce_all(): pl.pallas_call(functools.partial(reduce_kernel, shard_count, rep_count, p...  50.9 us
    dot_general x4, matrix products, project(): jnp.einsum('lsd,de->lse', inputs, weight, preferred_element_type=jnp.floa...  27.7 us
    dot_general x4, matrix products, project_back(): jnp.einsum('lse,de->lsd', gradient, weight, preferred_element_type=jnp.fl...  23.3 us
    ppermute x12, waiting for transfers between devices, to_shard(): lax.ppermute(values, 'shard', [(i, (i + hop) % shard_count) for i in rang...  19.9 us
    ppermute x12, starting transfers between devices, to_shard(): lax.ppermute(values, 'shard', [(i, (i + hop) % shard_count) for i in rang...  15.6 us
    dot_general x4, matrix products, weight_grad(): jnp.einsum('lsd,lse->de', inputs, gradient, preferred_element_type=jnp.fl...  13.1 us
    unnamed x180, local copies, waits for them, and re-layouts  12.9 us
    dot_general x1, matrix products, shards(): jnp.einsum('lqhd,lkhd->lhqk', attended_grad, value_rows, preferred_elemen...  10.8 us
  transfers between devices with their start and end apart: 14, of which 5 were waited for; matrix products, arithmetic and copies ran while one was open for 16% of the time, Pallas kernels for 0%

profile of v2, /device:TPU:0, one launch (start us, length us, event | category | flops | bytes accessed | tf_op | source)
XLA Modules:
  0.0 287.7 jit_solution(2261654365845177710)
XLA Ops:
  3.5 3.0 %collective-permute-start.2 = (bf16[10,384]{1,0:T(8,128)(2,1)}, bf16[10,384]{1,0:T(8,128)(2,1)S(1)}, u32[]{:S(2)}, u32[]{:S(2)}) collective-permute-start(bf16[10,384]{1,0:T(8,128)(2,1)} %constant_dynamic-update-slice_fusion), channel_id=1, source_target_pairs={{0,8},{8,16},{16,24},{24,0},{1,9},{9,17},{17,25},{25,1},{2,10},{10... | collective-permute-start | bytes 23048 | tf_op jit(solution)/shard_map/ppermute | solution.py:55
  6.5 2.6 collective-permute-start.1
  14.7 1.8 convert_reduce_fusion.4
  25.4 3.4 %collective-permute-start.3 = (f32[8,2304]{1,0:T(8,128)S(1)}, f32[8,2304]{1,0:T(8,128)S(1)}, u32[]{:S(2)}, u32[]{:S(2)}) collective-permute-start(f32[8,2304]{1,0:T(8,128)S(1)} %get-tuple-element.77), channel_id=1, source_target_pairs={{0,8},{8,16},{16,24},{24,0},{1,9},{9,17},{17,25},{25,1},{2,10},{10... | collective-permute-start | bytes 221192 | tf_op jit(solution)/shard_map/ppermute | solution.py:55
  31.7 2.3 collective-permute-start.6
  34.7 7.1 %collective-permute-done.4 = f32[8,2304]{1,0:T(8,128)S(1)} collective-permute-done((f32[8,2304]{1,0:T(8,128)S(1)}, f32[8,2304]{1,0:T(8,128)S(1)}, u32[]{:S(2)}, u32[]{:S(2)}) %collective-permute-start.4) | collective-permute-done | bytes 73760 | tf_op jit(solution)/shard_map/ppermute | solution.py:55
  41.9 1.7 pad_maximum_fusion.5
  43.6 1.6 convert_reduce_fusion.2
  45.9 2.6 fusion.20
  49.8 10.4 %collective-permute-done.11 = bf16[432,384]{1,0:T(8,128)(2,1)S(1)} collective-permute-done((bf16[432,384]{1,0:T(8,128)(2,1)}, bf16[432,384]{1,0:T(8,128)(2,1)S(1)}, u32[]{:S(2)}, u32[]{:S(2)}) %collective-permute-start.11) | collective-permute-done | bytes 331808 | tf_op jit(solution)/shard_map/ppermute | solution.py:55
  62.4 1.9 fusion.43
  65.2 4.6 %add_convert_fusion = bf16[8,256,1152]{2,1,0:T(8,128)(2,1)} fusion(f32[1152]{0:T(1024)S(1)} %copy-done.64, f32[8,384]{1,0:T(8,128)S(1)} %get-tuple-element.88, f32[8,384]{1,0:T(8,128)S(1)} %get-tuple-element.89, f32[8,256]{1,0:T(8,128)S(1)} %rsqrt.23, f32[8,256]{1,0:T(8,128)S(1)} %div.50, bf16[384,384]{1,0:T(8,128)(2,1)S(1)} %bitcast.252, ...), kind=kOutput, calls=%fused_computation.27 | convolution fusion | flops 1824030720 | bytes 7221760 | tf_op jit(solution)/shard_map/lsd,de->lse/dot_general | solution.py:31
  69.9 6.6 %copy.40 = bf16[8,256,1152]{1,2,0:T(8,128)(2,1)} copy(bf16[8,256,1152]{2,1,0:T(8,128)(2,1)} %add_convert_fusion) | data formatting | bytes 9437184 | tf_op jit(solution)/shard_map/convert_element_type | solution.py:390
  76.5 3.7 %multiply_reduce_fusion.1 = (f32[8,6,256]{2,1,0:T(8,128)S(1)}, f32[8,6,256,256]{2,3,1,0:T(8,128)S(1)}) fusion(bf16[8,256,3,6,64]{1,4,3,2,0:T(8,128)(2,1)} %bitcast.201), kind=kOutput, calls=%fused_computation.24 | convolution fusion | flops 408932352 | bytes 15777792 | tf_op jit(solution)/shard_map/lqhd,lkhd->lhqk/dot_general | solution.py:396
  80.3 2.6 exponential_reduce_fusion
  82.8 2.0 copy-done
  84.8 3.8 %convolution_convert_fusion.1 = bf16[8,6,64,256]{3,2,1,0:T(8,128)(2,1)S(1)} fusion(bf16[8,256,3,6,64]{1,4,3,2,0:T(8,128)(2,1)} %bitcast.202, f32[8,6,256,256]{2,3,1,0:T(8,128)S(1)} %get-tuple-element.104, f32[8,6,256]{2,1,0:T(8,128)S(1)} %log_add_fusion), kind=kOutput, calls=%fused_computation.84 | convolution fusion | flops 412876800 | bytes 15777792 | tf_op jit(solution)/shard_map/lhqk,lkhd->lqhd/dot_general | solution.py:402
  88.6 2.0 broadcast_select_fusion
  90.7 6.4 %fusion.24 = bf16[4,864,384]{2,1,0:T(8,128)(2,1)S(1)} fusion(s32[]{:T(128)S(6)} %select_n.60, bf16[1,864,384]{2,1,0:T(8,128)(2,1)S(1)} %bitcast.224, bf16[3,432,384]{2,1,0:T(8,128)(2,1)S(1)} %get-tuple-element.56, bf16[3,432,384]{2,1,0:T(8,128)(2,1)S(1)} %get-tuple-element.55), kind=kLoop, calls=%fused_computation.70 | loop fusion | flops 15925248 | bytes 5308420 | tf_op jit(solution)/shard_map/stack | solution.py:66
  99.3 3.0 %multiply_add_fusion = (f32[8,256,384]{2,1,0:T(8,128)S(1)}, f32[8,256,384]{2,1,0:T(8,128)}) fusion(f32[384]{0:T(512)S(1)} %copy-done.60, f32[8,384]{1,0:T(8,128)S(1)} %get-tuple-element.90, bf16[2048,384]{1,0:T(8,128)(2,1)S(1)} %copy-done.2, bf16[8,256,384]{1,2,0:T(8,128)(2,1)S(1)} %bitcast.210, bf16[384,384,1]{1,0,2:T(8,128)(2,1)S(1)} %bitcast.215), kind=kOutput, calls=%fused_computation.63 | convolution fusion | flops 607125504 | bytes 9745920 | tf_op jit(solution)/shard_map/lsd,de->lse/dot_general | solution.py:31
  104.7 9.3 %fusion.14 = (bf16[1536,8,256]{0,2,1:T(8,128)(2,1)}, f32[8,256,1536]{2,1,0:T(8,128)}) fusion(f32[1536]{0:T(1024)S(1)} %copy-done.62, bf16[384,384]{1,0:T(8,128)(2,1)S(1)} %bitcast.242, bf16[384,384]{1,0:T(8,128)(2,1)S(1)} %bitcast.244, bf16[384,384]{1,0:T(8,128)(2,1)S(1)} %bitcast.246, bf16[384,384]{1,0:T(8,128)(2,1)S(1)} %bitcast.240, ...), kind=kOutput, calls=%fused_computation.17 | convolution fusion | flops 2456027136 | bytes 23246848 | tf_op jit(solution)/shard_map/lsd,de->lse/dot_general | solution.py:31
  114.0 13.1 %convert_reduce_fusion = (f32[1536]{0:T(1024)}, bf16[8,256,1536]{2,1,0:T(8,128)(2,1)S(1)}) fusion(f32[8,256,1536]{2,1,0:T(8,128)} %get-tuple-element.112, f32[1536]{0:T(1024)S(1)} %copy-done.62, bf16[8,256,384]{2,1,0:T(8,128)(2,1)S(1)} %bitcast.226, bf16[1536,384,1]{1,0,2:T(8,128)(2,1)S(1)} %bitcast.234), kind=kOutput, calls=%fused_computation.18 | convolution fusion | flops 2488269312 | bytes 21639168 | tf_op jit(solution)/shard_map/lse,de->lsd/dot_general | solution.py:35
  127.1 4.3 %fusion.85 = (bf16[8,384]{1,0:T(8,128)(2,1)}, f32[8,256]{1,0:T(8,128)S(1)}, f32[8,256,384]{2,1,0:T(8,128)S(1)}) fusion(f32[8,384]{1,0:T(8,128)S(1)} %get-tuple-element.87, f32[8,256,384]{2,1,0:T(8,128)S(1)} %get-tuple-element.105, f32[8,256]{1,0:T(8,128)S(1)} %broadcast_multiply_fusion, bf16[8,256,1536]{2,1,0:T(8,128)(2,1)S(1)} %get-tuple-element.114, ...), kind=kOutput, calls=%fused_computation.217 | convolution fusion | flops 2424564736 | bytes 13797376 | tf_op jit(solution)/shard_map/lse,de->lsd/dot_general | solution.py:35
  131.4 4.1 %convolution_bitcast_fusion.1 = f32[384,1536]{1,0:T(8,128)} fusion(bf16[8,256,1536]{2,1,0:T(8,128)(2,1)S(1)} %get-tuple-element.114, f32[8,256,384]{2,1,0:T(8,128)S(1)} %get-tuple-element.105, f32[8,384]{1,0:T(8,128)S(1)} %get-tuple-element.86, f32[8,384]{1,0:T(8,128)S(1)} %get-tuple-element.87, f32[8,256]{1,0:T(8,128)S(1)} %fusion.68, ...), kind=kOutput, calls=%fused_computation.67 | convolution fusion | flops 2419851264 | bytes 11837440 | tf_op jit(solution)/shard_map/lsd,lse->de/dot_general | solution.py:39
  135.6 10.9 %multiply_reduce_fusion.2 = (bf16[8,384]{1,0:T(8,128)(2,1)}, f32[2048,384]{1,0:T(8,128)S(1)}, bf16[8,256,384]{2,1,0:T(8,128)(2,1)}, f32[8,256]{1,0:T(8,128)S(1)}, bf16[8,384]{1,0:T(8,128)(2,1)}) fusion(f32[384]{0:T(512)S(1)} %copy-done.70, bf16[2048,384]{1,0:T(8,128)(2,1)S(1)} %copy-done.23, f32[8,256,384]{2,1,0:T(8,128)S(1)} %get-tuple-element.105, ...), kind=kOutput, calls=%fused_computation.47 | convolution fusion | flops 2460737536 | bytes 26422784 | tf_op jit(solution)/shard_map/lsd,de->lse/dot_general | solution.py:31
  146.5 2.2 multiply_reduce_fusion.4
  148.7 1.7 copy-done.4
  152.1 2.3 convolution_convert_fusion
  154.4 1.9 copy.46
  156.3 8.2 %convolution_bitcast_fusion.2 = bf16[8,256,1,6,64]{1,4,3,0,2:T(8,128)(2,1)} fusion(bf16[8,256,6,64]{1,3,2,0:T(8,128)(2,1)S(1)} %bitcast.208, f32[8,6,256,256]{2,3,1,0:T(8,128)} %copy-done, f32[8,6,256]{2,1,0:T(8,128)S(1)} %log_add_fusion), kind=kOutput, calls=%fused_computation.76 | convolution fusion | flops 412090368 | bytes 15777792 | tf_op jit(solution)/shard_map/lhqk,lqhd->lkhd/dot_general | solution.py:436
  164.5 10.8 %multiply_reduce_fusion = (f32[8,6,256]{2,1,0:T(8,128)S(1)}, f32[8,6,256,256]{2,3,1,0:T(8,128)}) fusion(f32[8,6,256,256]{2,3,1,0:T(8,128)} %copy-done, f32[8,6,256]{2,1,0:T(8,128)S(1)} %log_add_fusion, bf16[8,256,6,64]{1,3,2,0:T(8,128)(2,1)S(1)} %bitcast.209, bf16[8,256,3,6,64]{1,4,3,2,0:T(8,128)(2,1)} %bitcast.203), kind=kOutput, calls=%fused_computation.20 | convolution fusion | flops 415223808 | bytes 28409856 | tf_op jit(solution)/shard_map/lqhd,lkhd->lhqk/dot_general | solution.py:442
  175.3 7.1 %multiply_convert_fusion = bf16[8,6,256,256]{2,3,1,0:T(8,128)(2,1)S(1)} fusion(f32[8,6,256,256]{2,3,1,0:T(8,128)} %get-tuple-element.109, f32[8,6,256,256]{2,3,1,0:T(8,128)S(1)} %bitcast.197, f32[8,6,256]{2,1,0:T(8,128)S(1)} %get-tuple-element.108, f32[8,6,256]{2,1,0:T(8,128)S(1)} %log_add_fusion), kind=kLoop, calls=%fused_computation.19 | loop fusion | flops 15728640 | bytes 31555584 | tf_op jit(solution)/shard_map/convert_element_type | solution.py:448
  182.4 3.2 %multiply_bitcast_fusion = bf16[8,256,1,6,64]{1,4,3,0,2:T(8,128)(2,1)} fusion(bf16[8,6,256,256]{2,3,1,0:T(8,128)(2,1)S(1)} %multiply_convert_fusion, bf16[8,256,3,6,64]{1,4,3,2,0:T(8,128)(2,1)S(1)} %bitcast.206), kind=kOutput, calls=%fused_computation.55 | convolution fusion | flops 404226048 | bytes 9437184 | tf_op jit(solution)/shard_map/lhqk,lqhd->lkhd/dot_general | solution.py:454
  185.6 2.4 multiply_bitcast_fusion.1
  188.0 1.5 fusion.88
  190.7 1.8 fusion.38
  192.6 3.9 %convert_reduce_fusion.1 = (f32[3,6,64]{2,1,0:T(8,128)S(1)}, bf16[8,256,3,6,64]{1,4,3,0,2:T(8,128)(2,1)}) fusion(bf16[8,256,1,6,64]{1,4,3,0,2:T(8,128)(2,1)} %convolution_bitcast_fusion.2, bf16[8,256,1,6,64]{1,4,3,0,2:T(8,128)(2,1)S(1)} %copy-done.8, bf16[8,256,1,6,64]{1,4,3,0,2:T(8,128)(2,1)S(1)} %copy-done.9), kind=kLoop, calls=%fused_computation.26 | loop fusion | flops 9436032 | bytes 9441792 | tf_op jit(solution)/shard_map/reduce_sum | solution.py:43
  197.4 2.9 copy.50
  200.4 3.7 %fusion.84 = (bf16[8,384]{1,0:T(8,128)(2,1)S(1)}, f32[8,256]{1,0:T(8,128)S(1)}, f32[8,256,384]{2,1,0:T(8,128)S(1)}) fusion(f32[8,384]{1,0:T(8,128)S(1)} %get-tuple-element.89, f32[8,256]{1,0:T(8,128)S(1)} %copy-done.52, bf16[8,256,1152]{1,2,0:T(8,128)(2,1)S(1)} %bitcast.212, bf16[384,384]{1,0:T(8,128)(2,1)S(1)} %bitcast.253, ...), kind=kOutput, calls=%fused_computation.216 | convolution fusion | flops 1819307008 | bytes 10356736 | tf_op jit(solution)/shard_map/lse,de->lsd/dot_general | solution.py:35
  204.2 2.3 convolution_bitcast_fusion
  208.0 4.9 %fusion.27.refs_0_ = f32[4,384,384]{2,1,0:T(8,128)} fusion(bf16[8,256,384,1]{2,1,0,3:T(8,128)(2,1)S(1)} %bitcast.227, bf16[8,32,4,8,384]{4,3,2,1,0:T(8,128)(2,1)S(1)} %bitcast.263), kind=kOutput, calls=%fused_computation.85 | convolution fusion | flops 2415919104 | bytes 10223616 | tf_op jit(solution)/shard_map/lsd,lse->de/dot_general | solution.py:39
  212.9 2.2 multiply_reduce_fusion.5
  215.1 1.6 pad_maximum_fusion.refs_1_
  216.8 1.5 pad_maximum_fusion.1.refs_2_
  219.0 50.9 %shard_map.228 = (f32[384,384]{1,0:T(8,128)}, f32[384,384]{1,0:T(8,128)}, f32[384,384]{1,0:T(8,128)}, f32[8,128]{1,0:T(8,128)}, bf16[32,16,1408]{2,1,0:T(8,128)(2,1)}, /*index=5*/f32[4,8,128]{2,1,0:T(8,128)}) custom-call(f32[4,384,384]{2,1,0:T(8,128)} %fusion.27.refs_0_, f32[4,384,384]{2,1,0:T(8,128)} %pad_maximum_fusion.refs_1_, ...), custom_call_target="tpu_custom_call" | custom-call | tf_op jit(solution)/shard_map/pallas_call | solution.py:309
  274.8 2.3 fusion.90
  277.1 2.4 add_add_fusion.2
  281.9 1.4 fusion.55
  (282 shorter events, 47.9 us)
Async XLA Ops:
  0.6 15.8 %copy-start.1 = (bf16[2048,384]{1,0:T(8,128)(2,1)S(1)}, bf16[2048,384]{1,0:T(8,128)(2,1)}, u32[]{:S(2)}) copy-start(bf16[2048,384]{1,0:T(8,128)(2,1)} %param.13) | copy-start | bytes 4718596
  0.7 17.2 %copy-start.50 = (bf16[96,384]{1,0:T(8,128)(2,1)S(1)}, bf16[96,384]{1,0:T(8,128)(2,1)}, u32[]{:S(2)}) copy-start(bf16[96,384]{1,0:T(8,128)(2,1)} %param.19) | copy-start | bytes 221188
  0.7 17.3 %copy-start.44 = (bf16[96,1536]{1,0:T(8,128)(2,1)S(1)}, bf16[96,1536]{1,0:T(8,128)(2,1)}, u32[]{:S(2)}) copy-start(bf16[96,1536]{1,0:T(8,128)(2,1)} %param.21) | copy-start | bytes 884740
  0.7 17.9 %copy-start.45 = (bf16[384,384]{1,0:T(8,128)(2,1)S(1)}, bf16[384,384]{1,0:T(8,128)(2,1)}, u32[]{:S(2)}) copy-start(bf16[384,384]{1,0:T(8,128)(2,1)} %param.23) | copy-start | bytes 884740
  3.5 17.7 %collective-permute-start.2 = (bf16[10,384]{1,0:T(8,128)(2,1)}, bf16[10,384]{1,0:T(8,128)(2,1)S(1)}, u32[]{:S(2)}, u32[]{:S(2)}) collective-permute-start(bf16[10,384]{1,0:T(8,128)(2,1)} %constant_dynamic-update-slice_fusion), channel_id=1, source_target_pairs={{0,8},{8,16},{16,24},{24,0},{1,9},{9,17},{17,25},{25,1},{2,10},{10... | collective-permute-start | bytes 23048 | tf_op jit(solution)/shard_map/ppermute | solution.py:55
  6.5 14.7 %collective-permute-start.1 = (bf16[10,384]{1,0:T(8,128)(2,1)}, bf16[10,384]{1,0:T(8,128)(2,1)S(1)}, u32[]{:S(2)}, u32[]{:S(2)}) collective-permute-start(bf16[10,384]{1,0:T(8,128)(2,1)} %constant_dynamic-update-slice_fusion), channel_id=1, source_target_pairs={{0,16},{8,24},{16,0},{24,8},{1,17},{9,25},{17,1},{25,9},{2,18},{10... | collective-permute-start | bytes 23048 | tf_op jit(solution)/shard_map/ppermute | solution.py:55
  9.1 11.4 %collective-permute-start = (bf16[10,384]{1,0:T(8,128)(2,1)}, bf16[10,384]{1,0:T(8,128)(2,1)}, u32[]{:S(2)}, u32[]{:S(2)}) collective-permute-start(bf16[10,384]{1,0:T(8,128)(2,1)} %constant_dynamic-update-slice_fusion), channel_id=1, source_target_pairs={{0,24},{8,0},{16,8},{24,16},{1,25},{9,1},{17,9},{25,17},{2,26},{10... | collective-permute-start | bytes 23048 | tf_op jit(solution)/shard_map/ppermute | solution.py:55
  11.4 8.0 %copy-start.69 = (bf16[576]{0:T(1024)(128)(2,1)S(1)}, bf16[576]{0:T(1024)(128)(2,1)}, u32[]{:S(2)}) copy-start(bf16[576]{0:T(1024)(128)(2,1)} %param.16) | copy-start | bytes 3460
  11.4 8.2 %copy-start.20 = (bf16[96,2304]{1,0:T(8,128)(2,1)S(1)}, bf16[96,2304]{1,0:T(8,128)(2,1)}, u32[]{:S(2)}) copy-start(bf16[96,2304]{1,0:T(8,128)(2,1)} %param.15) | copy-start | bytes 1327108
  12.9 28.9 %collective-permute-start.8 = (bf16[144,384]{1,0:T(8,128)(2,1)}, bf16[144,384]{1,0:T(8,128)(2,1)S(1)}, u32[]{:S(2)}, u32[]{:S(2)}) collective-permute-start(bf16[144,384]{1,0:T(8,128)(2,1)} %constant_dynamic-slice_fusion.1), channel_id=1, source_target_pairs={{0,8},{8,16},{16,24},{24,0},{1,9},{9,17},{17,25},{25,1},{2,10},{10... | collective-permute-start | bytes 331784 | tf_op jit(solution)/shard_map/ppermute | solution.py:55
  13.5 28.3 %collective-permute-start.7 = (bf16[144,384]{1,0:T(8,128)(2,1)}, bf16[144,384]{1,0:T(8,128)(2,1)}, u32[]{:S(2)}, u32[]{:S(2)}) collective-permute-start(bf16[144,384]{1,0:T(8,128)(2,1)} %constant_dynamic-slice_fusion.1), channel_id=1, source_target_pairs={{0,16},{8,24},{16,0},{24,8},{1,17},{9,25},{17,1},{25,9},{2,18},{10... | collective-permute-start | bytes 331784 | tf_op jit(solution)/shard_map/ppermute | solution.py:55
  14.7 10.4 %copy-start.46 = (bf16[8,384]{1,0:T(8,128)(2,1)S(1)}, bf16[8,384]{1,0:T(8,128)(2,1)}, u32[]{:S(2)}) copy-start(bf16[8,384]{1,0:T(8,128)(2,1)} %param.14) | copy-start | bytes 18436
  19.6 44.9 %copy-start.51 = (f32[8,256]{1,0:T(8,128)}, f32[8,256]{1,0:T(8,128)S(1)}, u32[]{:S(2)}) copy-start(f32[8,256]{1,0:T(8,128)S(1)} %div.50) | copy-start | bytes 24580
  19.6 4.7 %copy-start.48 = (f32[8,256]{1,0:T(8,128)}, f32[8,256]{1,0:T(8,128)S(1)}, u32[]{:S(2)}) copy-start(f32[8,256]{1,0:T(8,128)S(1)} %add.193) | copy-start | bytes 24580
  19.6 44.8 %copy-start.53 = (f32[8,256]{1,0:T(8,128)}, f32[8,256]{1,0:T(8,128)S(1)}, u32[]{:S(2)}) copy-start(f32[8,256]{1,0:T(8,128)S(1)} %rsqrt.23) | copy-start | bytes 24580
  24.3 19.3 %copy-start.22 = (bf16[2048,384]{1,0:T(8,128)(2,1)S(1)}, bf16[2048,384]{1,0:T(8,128)(2,1)}, u32[]{:S(2)}) copy-start(bf16[2048,384]{1,0:T(8,128)(2,1)} %param.25) | copy-start | bytes 4718596
  25.4 6.3 %collective-permute-start.3 = (f32[8,2304]{1,0:T(8,128)S(1)}, f32[8,2304]{1,0:T(8,128)S(1)}, u32[]{:S(2)}, u32[]{:S(2)}) collective-permute-start(f32[8,2304]{1,0:T(8,128)S(1)} %get-tuple-element.77), channel_id=1, source_target_pairs={{0,8},{8,16},{16,24},{24,0},{1,9},{9,17},{17,25},{25,1},{2,10},{10... | collective-permute-start | bytes 221192 | tf_op jit(solution)/shard_map/ppermute | solution.py:55
  28.9 5.5 %collective-permute-start.5 = (f32[8,2304]{1,0:T(8,128)S(1)}, f32[8,2304]{1,0:T(8,128)S(1)}, u32[]{:S(2)}, u32[]{:S(2)}) collective-permute-start(f32[8,2304]{1,0:T(8,128)S(1)} %get-tuple-element.78), channel_id=1, source_target_pairs={{0,24},{8,0},{16,8},{24,16},{1,25},{9,1},{17,9},{25,17},{2,26},{10... | collective-permute-start | bytes 221192 | tf_op jit(solution)/shard_map/ppermute | solution.py:55
  29.3 12.4 %collective-permute-start.4 = (f32[8,2304]{1,0:T(8,128)S(1)}, f32[8,2304]{1,0:T(8,128)S(1)}, u32[]{:S(2)}, u32[]{:S(2)}) collective-permute-start(f32[8,2304]{1,0:T(8,128)S(1)} %get-tuple-element.79), channel_id=1, source_target_pairs={{0,16},{8,24},{16,0},{24,8},{1,17},{9,25},{17,1},{25,9},{2,18},{10... | collective-permute-start | bytes 221192 | tf_op jit(solution)/shard_map/ppermute | solution.py:55
  31.7 10.1 %collective-permute-start.6 = (bf16[144,384]{1,0:T(8,128)(2,1)}, bf16[144,384]{1,0:T(8,128)(2,1)S(1)}, u32[]{:S(2)}, u32[]{:S(2)}) collective-permute-start(bf16[144,384]{1,0:T(8,128)(2,1)} %constant_dynamic-slice_fusion.1), channel_id=1, source_target_pairs={{0,24},{8,0},{16,8},{24,16},{1,25},{9,1},{17,9},{25,17},{2,26},{10... | collective-permute-start | bytes 331784 | tf_op jit(solution)/shard_map/ppermute | solution.py:55
  34.3 15.5 %collective-permute-start.12 = (bf16[432,384]{1,0:T(8,128)(2,1)}, bf16[432,384]{1,0:T(8,128)(2,1)S(1)}, u32[]{:S(2)}, u32[]{:S(2)}) collective-permute-start(bf16[432,384]{1,0:T(8,128)(2,1)} %constant_dynamic-slice_fusion), channel_id=1, source_target_pairs={{0,8},{8,16},{16,24},{24,0},{1,9},{9,17},{17,25},{25,1},{2,10},{10... | collective-permute-start | bytes 995336 | tf_op jit(solution)/shard_map/ppermute | solution.py:55
  41.7 18.5 %collective-permute-start.11 = (bf16[432,384]{1,0:T(8,128)(2,1)}, bf16[432,384]{1,0:T(8,128)(2,1)S(1)}, u32[]{:S(2)}, u32[]{:S(2)}) collective-permute-start(bf16[432,384]{1,0:T(8,128)(2,1)} %constant_dynamic-slice_fusion), channel_id=1, source_target_pairs={{0,16},{8,24},{16,0},{24,8},{1,17},{9,25},{17,1},{25,9},{2,18},{10... | collective-permute-start | bytes 995336 | tf_op jit(solution)/shard_map/ppermute | solution.py:55
  41.8 18.4 %collective-permute-start.10 = (bf16[432,384]{1,0:T(8,128)(2,1)}, bf16[432,384]{1,0:T(8,128)(2,1)S(1)}, u32[]{:S(2)}, u32[]{:S(2)}) collective-permute-start(bf16[432,384]{1,0:T(8,128)(2,1)} %constant_dynamic-slice_fusion), channel_id=1, source_target_pairs={{0,24},{8,0},{16,8},{24,16},{1,25},{9,1},{17,9},{25,17},{2,26},{10... | collective-permute-start | bytes 995336 | tf_op jit(solution)/shard_map/ppermute | solution.py:55
  43.5 17.8 %collective-permute-start.9 = (bf16[3,144,384]{2,1,0:T(8,128)(2,1)}, bf16[3,144,384]{2,1,0:T(8,128)(2,1)}, u32[]{:S(2)}, u32[]{:S(2)}) collective-permute-start(bf16[3,144,384]{2,1,0:T(8,128)(2,1)} %pad_maximum_fusion.5), channel_id=1, source_target_pairs={{0,1},{1,0},{2,3},{3,2},{4,5},{5,4},{6,7},{7,6},{8,9},{9,8},{10,11... | collective-permute-start | bytes 995336 | tf_op jit(solution)/shard_map/ppermute | solution.py:51
  43.5 4.9 %copy-start.56 = (f32[8,384]{1,0:T(8,128)}, f32[8,384]{1,0:T(8,128)S(1)}, u32[]{:S(2)}) copy-start(f32[8,384]{1,0:T(8,128)S(1)} %get-tuple-element.85) | copy-start | bytes 36868
  45.9 16.5 %copy-start.29 = (bf16[1,288,384]{2,1,0:T(8,128)(2,1)S(1)}, bf16[1,288,384]{2,1,0:T(8,128)(2,1)}, u32[]{:S(2)}) copy-start(bf16[1,288,384]{2,1,0:T(8,128)(2,1)} %get-tuple-element.81) | copy-start | bytes 663556
  60.2 5.0 %copy-start.64 = (f32[1152]{0:T(1024)S(1)}, f32[1152]{0:T(1024)}, u32[]{:S(2)}) copy-start(f32[1152]{0:T(1024)} %maximum_convert_fusion.2) | copy-start | bytes 13828
  61.3 27.3 %collective-permute-start.13 = (bf16[3,432,384]{2,1,0:T(8,128)(2,1)}, bf16[3,432,384]{2,1,0:T(8,128)(2,1)}, u32[]{:S(2)}, u32[]{:S(2)}) collective-permute-start(bf16[3,432,384]{2,1,0:T(8,128)(2,1)} %pad_maximum_fusion.2), channel_id=1, source_target_pairs={{0,1},{1,0},{2,3},{3,2},{4,5},{5,4},{6,7},{7,6},{8,9},{9,8},{10,11... | collective-permute-start | bytes 2985992 | tf_op jit(solution)/shard_map/ppermute | solution.py:51
  64.4 5.4 %copy-start.38 = (bf16[4,96,384]{2,1,0:T(8,128)(2,1)}, bf16[4,96,384]{2,1,0:T(8,128)(2,1)S(1)}, u32[]{:S(2)}) copy-start(bf16[4,96,384]{2,1,0:T(8,128)(2,1)S(1)} %get-tuple-element.64) | copy-start | bytes 884740
  80.2 4.6 %copy-start = (f32[8,6,256,256]{2,3,1,0:T(8,128)}, f32[8,6,256,256]{2,3,1,0:T(8,128)S(1)}, u32[]{:S(2)}) copy-start(f32[8,6,256,256]{2,3,1,0:T(8,128)S(1)} %get-tuple-element.104) | copy-start | bytes 37748740
  88.6 10.7 %copy-start.12 = (bf16[8,6,64,256]{3,2,1,0:T(8,128)(2,1)}, bf16[8,6,64,256]{3,2,1,0:T(8,128)(2,1)S(1)}, u32[]{:S(2)}) copy-start(bf16[8,6,64,256]{3,2,1,0:T(8,128)(2,1)S(1)} %convolution_convert_fusion.1) | copy-start | bytes 4718596
  104.7 9.3 %copy-start.24 = (bf16[2048,384]{1,0:T(8,128)(2,1)S(1)}, bf16[2048,384]{1,0:T(8,128)(2,1)}, u32[]{:S(2)}) copy-start(bf16[2048,384]{1,0:T(8,128)(2,1)} %get-tuple-element.42) | copy-start | bytes 4718596
  104.7 9.3 %copy-start.28 = (bf16[4,384,384]{2,1,0:T(8,128)(2,1)S(1)}, bf16[4,384,384]{2,1,0:T(8,128)(2,1)}, u32[]{:S(2)}) copy-start(bf16[4,384,384]{2,1,0:T(8,128)(2,1)} %slice.249) | copy-start | bytes 3538948
  131.4 4.2 %copy-start.23 = (bf16[2048,384]{1,0:T(8,128)(2,1)S(1)}, bf16[2048,384]{1,0:T(8,128)(2,1)}, u32[]{:S(2)}) copy-start(bf16[2048,384]{1,0:T(8,128)(2,1)} %param.25) | copy-start | bytes 4718596
  131.4 4.2 %copy-start.57 = (f32[8,384]{1,0:T(8,128)S(1)}, f32[8,384]{1,0:T(8,128)}, u32[]{:S(2)}) copy-start(f32[8,384]{1,0:T(8,128)} %copy-done.56) | copy-start | bytes 36868
  131.4 4.2 %copy-start.70 = (f32[384]{0:T(512)S(1)}, f32[384]{0:T(512)}, u32[]{:S(2)}) copy-start(f32[384]{0:T(512)} %reshape.348) | copy-start | bytes 4612
  135.6 10.9 %copy-start.6 = (f32[8,256,384]{2,1,0:T(8,128)S(1)}, f32[8,256,384]{2,1,0:T(8,128)}, u32[]{:S(2)}) copy-start(f32[8,256,384]{2,1,0:T(8,128)} %get-tuple-element.106) | copy-start | bytes 9437188
  135.6 10.9 %copy-start.61 = (f32[384]{0:T(512)S(1)}, f32[384]{0:T(512)}, u32[]{:S(2)}) copy-start(f32[384]{0:T(512)} %reshape.346) | copy-start | bytes 4612
  156.3 19.0 %slice-start = ((s8[12582912]{0:T(1024)(128)(4,1)}), s8[4194304]{0:T(1024)(128)(4,1)S(1)}, s32[]{:S(2)}) async-start(s8[12582912]{0:T(1024)(128)(4,1)} %bitcast.196), calls=%async_computation | async-start | bytes 8388608
  156.3 19.0 %slice-start.1 = ((s8[12582912]{0:T(1024)(128)(4,1)}), s8[4194304]{0:T(1024)(128)(4,1)S(1)}, s32[]{:S(2)}) async-start(s8[12582912]{0:T(1024)(128)(4,1)} %bitcast.196), calls=%async_computation.1 | async-start | bytes 8388608
  164.5 10.8 %slice-start.2 = ((s8[12582912]{0:T(1024)(128)(4,1)}), s8[4194304]{0:T(1024)(128)(4,1)S(1)}, s32[]{:S(2)}) async-start(s8[12582912]{0:T(1024)(128)(4,1)} %bitcast.196), calls=%async_computation.2 | async-start | bytes 8388608
  164.5 17.9 %slice-start.3 = ((s8[4718592]{0:T(1024)(128)(4,1)}), s8[4194304]{0:T(1024)(128)(4,1)S(1)}, s32[]{:S(2)}) async-start(s8[4718592]{0:T(1024)(128)(4,1)} %bitcast.204), calls=%async_computation.3 | async-start | bytes 8388608
  175.3 7.1 %slice-start.4 = ((s8[4718592]{0:T(1024)(128)(4,1)}), s8[524288]{0:T(1024)(128)(4,1)S(1)}, s32[]{:S(2)}) async-start(s8[4718592]{0:T(1024)(128)(4,1)} %bitcast.204), calls=%async_computation.4 | async-start | bytes 1048576
  208.0 4.9 %copy-start.54 = (f32[8,256]{1,0:T(8,128)S(1)}, f32[8,256]{1,0:T(8,128)}, u32[]{:S(2)}) copy-start(f32[8,256]{1,0:T(8,128)} %copy-done.53) | copy-start | bytes 24580
  219.0 58.1 %copy-start.5 = (f32[8,256,384]{2,1,0:T(8,128)S(1)}, f32[8,256,384]{2,1,0:T(8,128)}, u32[]{:S(2)}) copy-start(f32[8,256,384]{2,1,0:T(8,128)} %copy-done.4) | copy-start | bytes 9437188
  279.6 4.4 %copy-start.32 = (f32[384,384]{1,0:T(8,128)S(1)}, f32[384,384]{1,0:T(8,128)}, u32[]{:S(2)}) copy-start(f32[384,384]{1,0:T(8,128)} %get-tuple-element.23) | copy-start | bytes 1769476
  279.6 4.4 %copy-start.33 = (f32[384,384]{1,0:T(8,128)S(1)}, f32[384,384]{1,0:T(8,128)}, u32[]{:S(2)}) copy-start(f32[384,384]{1,0:T(8,128)} %get-tuple-element.21) | copy-start | bytes 1769476
  281.9 4.5 %copy-start.31 = (f32[384,384]{1,0:T(8,128)S(1)}, f32[384,384]{1,0:T(8,128)}, u32[]{:S(2)}) copy-start(f32[384,384]{1,0:T(8,128)} %get-tuple-element.143) | copy-start | bytes 1769476
  (44 other events, 97.3 us)
